TPU v7x, 32 devices: a whole 2x2x4 slice. The times are simulated.
32 devices in a mesh: pipe: 2 (over core), seq: 4 (over y, x), tensor: 4 (over z).
Axes of the slice: x: 2, y: 2, z: 4, core: 2. Of those that a mesh axis runs over, the one named last changes fastest.
Arguments:
- tokens: float32 [4, 4096, 800], P(None, 'seq'), may hold values from -6 to 6
- segments: int32 [4, 4096], P(None, 'seq'), may hold values from 0 to 15, as said below
- pad_mask: int32 [4, 4096], P(None, 'seq'), may hold values from 0 to 1, as said below
- cotangent: float32 [4, 4096, 800], P(None, 'seq'), may hold values from -6 to 6
- gain_first: float32 [2, 800], P('pipe'), may hold values from 0.1 to 1.9
- bias_first: float32 [2, 800], P('pipe'), may hold values from -3 to 3
- weight_inner: float32 [2, 800, 400], P('pipe', None, 'tensor'), may hold values from -0.21875 to 0.21875
- bias_inner: float32 [2, 400], P('pipe', 'tensor'), may hold values from -3 to 3
- gain_middle: float32 [2, 400], P('pipe', 'tensor'), may hold values from 0.1 to 1.9
- bias_middle: float32 [2, 400], P('pipe', 'tensor'), may hold values from -3 to 3
- weight_conv_encoder: float32 [5, 400, 400], P(None, None, 'tensor'), may hold values from -0.125 to 0.125
- weight_conv_decoder: float32 [3, 400, 400], P(None, None, 'tensor'), may hold values from -0.1875 to 0.1875
- bias_conv: float32 [2, 400], P('pipe', 'tensor'), may hold values from -3 to 3
- gain_last: float32 [2, 400], P('pipe', 'tensor'), may hold values from 0.1 to 1.9
- bias_last: float32 [2, 400], P('pipe', 'tensor'), may hold values from -3 to 3
- weight_outer: float32 [2, 400, 800], P('pipe', 'tensor'), may hold values from -0.3125 to 0.3125
- bias_outer: float32 [2, 800], P('pipe'), may hold values from -3 to 3
Outputs:
- section_output: float32 [2, 4, 4096, 800], P('pipe', None, 'seq')
- input_gradient: float32 [2, 4, 4096, 800], P('pipe', None, 'seq')
- grad_gain_first: float32 [2, 800], P('pipe')
- grad_bias_first: float32 [2, 800], P('pipe')
- grad_weight_inner: float32 [2, 800, 400], P('pipe', None, 'tensor')
- grad_bias_inner: float32 [2, 400], P('pipe', 'tensor')
- grad_gain_middle: float32 [2, 400], P('pipe', 'tensor')
- grad_bias_middle: float32 [2, 400], P('pipe', 'tensor')
- grad_conv_encoder: float32 [5, 400, 400], P(None, None, 'tensor')
- grad_conv_decoder: float32 [3, 400, 400], P(None, None, 'tensor')
- grad_bias_conv: float32 [2, 400], P('pipe', 'tensor')
- grad_gain_last: float32 [2, 400], P('pipe', 'tensor')
- grad_bias_last: float32 [2, 400], P('pipe', 'tensor')
- grad_weight_outer: float32 [2, 400, 800], P('pipe', 'tensor')
- grad_bias_outer: float32 [2, 800], P('pipe')
Inputs may be any that keep to these rules, and one draw needn't show every extreme that they name: `segments`: along each row segment numbers start at 0 and never fall, rising by at most one; some row of every draw reaches 15. In every draw one row holds a segment that begins within its first 64 positions and lasts to the row's end. `pad_mask`: each row is 1 up to a padded tail of fewer than 64 positions, which are 0.
All inputs are finite; a program needn't handle non-finite values.
Results may differ from a plain program's by a relative error of at most 0.015.
Values may be sent and summed in bfloat16 or wider, within the bound.
No kernel may reach another device: no remote copies, remote signals or barrier semaphores. Data moves between devices by JAX's collectives and lax.ppermute only.
A program may use at most 320 MiB of HBM per device.

v0:
```python
import jax
import jax.numpy as jnp
from jax import lax
from jax.sharding import PartitionSpec as P

ENCODER_SPACING = 16
MICRO = 4


EPSILON = 1e-05


def padded(cells, sides, width):
    for axis, dim in sides:
        count = lax.axis_size(axis)
        ends = count - 1
        head = lax.slice_in_dim(cells, 0, width, axis=dim)
        tail = lax.slice_in_dim(cells, cells.shape[dim] - width, cells.shape[dim], axis=dim)
        cells = jnp.concatenate(
            [
                lax.ppermute(tail, axis, [(i, (i + 1) % count) for i in range(ends)]),
                cells,
                lax.ppermute(head, axis, [((i + 1) % count, i) for i in range(ends)]),
            ],
            axis=dim,
        )
    return cells


def shifted_2(x, axis, by):
    peers = lax.axis_size(axis)
    pairs = [(i, i + by) for i in range(peers) if 0 <= i + by < peers]
    return lax.ppermute(x, axis, pairs)


def as_sent(x):
    return jax.tree.map(lambda a: a.astype(jnp.bfloat16) if a.dtype == jnp.float32 else a, x)


def smooth(values):
    return jax.nn.gelu(values, approximate=True)


def smooth_back(normed, grad):
    _, back = jax.vjp(smooth, normed)
    return back(grad)[0]


def pair_sum(first, second):
    return lax.psum((first, second), "tensor")


def widen(values, receptive_span):
    return padded(values, (("seq", 1),), receptive_span)


def norm_whole(values, gain, bias):
    center = jnp.mean(values, axis=-1, keepdims=True)
    spread = jnp.mean(values * values, axis=-1, keepdims=True) - center * center
    inverse = lax.rsqrt(spread + EPSILON)
    scaled = (values - center) * inverse
    return (scaled * gain + bias, scaled, inverse)


def norm_shared(values, gain, bias, width):
    total, squares = pair_sum(jnp.sum(values, axis=-1), jnp.sum(values * values, axis=-1))
    center = (total / width)[..., None]
    spread = (squares / width)[..., None] - center * center
    inverse = lax.rsqrt(spread + EPSILON)
    scaled = (values - center) * inverse
    return (scaled * gain + bias, scaled, inverse)


def back_whole(grad, scaled, inverse, gain):
    weighted = grad * gain
    first_mean = jnp.mean(weighted, axis=-1, keepdims=True)
    second_mean = jnp.mean(weighted * scaled, axis=-1, keepdims=True)
    return inverse * (weighted - first_mean - scaled * second_mean)


def back_shared(grad, scaled, inverse, gain, width):
    weighted = grad * gain
    total, cross = pair_sum(jnp.sum(weighted, axis=-1), jnp.sum(weighted * scaled, axis=-1))
    return inverse * (weighted - (total / width)[..., None] - scaled * (cross / width)[..., None])


def tap_masks(codes_local, codes_wide, tap_shifts, receptive_span, sign, kernel_taps):
    length = codes_local.shape[1]
    masks = []
    for tap_number in range(kernel_taps):
        shifted = lax.dynamic_slice_in_dim(
            codes_wide, receptive_span + sign * tap_shifts[tap_number], length, 1
        )
        masks.append((shifted == codes_local).astype(jnp.bfloat16))
    return masks


def on_device(
    tokens,
    segments,
    pad_mask,
    cotangent,
    gain_first,
    bias_first,
    weight_inner,
    bias_inner,
    gain_middle,
    bias_middle,
    weight_conv_encoder,
    weight_conv_decoder,
    bias_conv,
    gain_last,
    bias_last,
    weight_outer,
    bias_outer,
):
    block_portion = lax.axis_index("pipe")
    rows_all, length, width = tokens.shape
    group = rows_all // MICRO
    receptive_span = 2 * ENCODER_SPACING
    kernel_taps = weight_conv_encoder.shape[0]
    dec_taps = weight_conv_decoder.shape[0]
    inner = weight_conv_encoder.shape[1]
    local_inner = weight_conv_encoder.shape[2]
    params = tuple(
        (
            p[0]
            for p in (
                gain_first,
                bias_first,
                weight_inner,
                bias_inner,
                gain_middle,
                bias_middle,
                bias_conv,
                gain_last,
                bias_last,
                weight_outer,
                bias_outer,
            )
        )
    )
    (
        first_scale,
        first_shift,
        inner_matrix,
        inner_shift,
        middle_scale,
        middle_shift,
        conv_shift,
        last_scale,
        last_shift,
        outer_matrix,
        outer_shift,
    ) = params
    inner_low = inner_matrix.astype(jnp.bfloat16)
    outer_low = outer_matrix.astype(jnp.bfloat16)
    encoder_low = weight_conv_encoder.astype(jnp.bfloat16)
    decoder_low = jnp.concatenate(
        [
            jnp.zeros((kernel_taps - dec_taps, inner, local_inner), jnp.bfloat16),
            weight_conv_decoder.astype(jnp.bfloat16),
        ],
        axis=0,
    )
    conv_low = jnp.where(block_portion == 0, encoder_low, decoder_low)
    step_total = jnp.arange(kernel_taps, dtype=jnp.int32)
    tap_shifts = jnp.where(
        block_portion == 0, ENCODER_SPACING * (step_total - 2), step_total - (kernel_taps - 1)
    )
    codes = jnp.where(pad_mask == 1, segments + 1, 0)
    codes_wide = padded(codes, (("seq", 1),), receptive_span)
    keep = pad_mask.astype(jnp.float32)

    def rows_of(array, index):
        return array[index * group : (index + 1) * group]

    def choose(array, tick):
        early = rows_of(array, min(tick, MICRO - 1))
        late = rows_of(array, max(tick - 1, 0))
        return jnp.where(block_portion == 0, early, late)

    def forward(inputs, codes_local, codes_pad, keep_local, finish):
        normed_first, scaled_first, inverse_first = norm_whole(inputs, first_scale, first_shift)
        first = smooth(normed_first).astype(jnp.bfloat16)
        hidden = (
            jnp.einsum("rtd,dh->rth", first, inner_low, preferred_element_type=jnp.float32)
            + inner_shift
        )
        normed_second, scaled_second, inverse_second = norm_shared(
            hidden, middle_scale, middle_shift, inner
        )
        second = smooth(normed_second).astype(jnp.bfloat16)
        second_pad = widen(second, receptive_span)
        masks = tap_masks(codes_local, codes_pad, tap_shifts, receptive_span, 1, kernel_taps)
        empty = jnp.zeros((group, length, local_inner), jnp.float32)
        total = empty
        piece = lax.all_gather(second_pad, "tensor", axis=2, tiled=True)
        for tap_number in range(kernel_taps):
            shifted = (
                lax.dynamic_slice_in_dim(piece, receptive_span + tap_shifts[tap_number], length, 1)
                * masks[tap_number][..., None]
            )
            matrix = conv_low[tap_number]
            total = total + jnp.einsum(
                "rtc,co->rto", shifted, matrix, preferred_element_type=jnp.float32
            )
        mixed = total + conv_shift
        normed_third, scaled_third, inverse_third = norm_shared(
            mixed, last_scale, last_shift, inner
        )
        third = smooth(normed_third).astype(jnp.bfloat16)
        saved = (
            normed_first,
            scaled_first,
            inverse_first,
            first,
            normed_second,
            scaled_second,
            inverse_second,
            second_pad,
            normed_third,
            scaled_third,
            inverse_third,
            third,
        )
        if not finish:
            return (None, saved)
        partial_out = jnp.einsum(
            "rth,hd->rtd", third, outer_low, preferred_element_type=jnp.float32
        )
        product = lax.psum(partial_out, "tensor")
        output = inputs + (product + outer_shift) * keep_local[..., None]
        return (output, saved)

    received = jnp.zeros((group, length, width), jnp.float32)
    output_list, input_list, kept_list = ([], [], [])
    for tick in range(MICRO + 1):
        inputs = jnp.where(block_portion == 0, rows_of(tokens, min(tick, MICRO - 1)), received)
        output, saved = forward(
            inputs, choose(codes, tick), choose(codes_wide, tick), choose(keep, tick), True
        )
        output_list.append(output)
        input_list.append(inputs)
        if tick < MICRO:
            received = shifted_2(output, "pipe", 1)
    totals = tuple((jnp.zeros(p.shape, jnp.float32) for p in params))
    conv_total = jnp.zeros((kernel_taps, inner, local_inner), jnp.float32)
    back_received = jnp.zeros((group, length, width), jnp.float32)
    grad_list = []
    for tick in range(MICRO + 1):
        index = MICRO - tick
        codes_local = choose(codes, index)
        codes_pad = choose(codes_wide, index)
        keep_local = choose(keep, index)
        grad_out = jnp.where(
            block_portion == 1, rows_of(cotangent, max(MICRO - 1 - tick, 0)), back_received
        )
        saved = forward(input_list[index], codes_local, codes_pad, keep_local, False)[1]
        (
            backward_normed_first,
            backward_scaled_first,
            backward_inverse_first,
            backward_first,
            backward_normed_second,
            backward_scaled_second,
            backward_inverse_second,
            backward_second_pad,
            backward_normed_third,
            backward_scaled_third,
            backward_inverse_third,
            backward_third,
        ) = saved
        branch = grad_out * keep_local[..., None]
        grad_outer_shift = jnp.sum(branch, axis=(0, 1))
        branch_low = branch.astype(jnp.bfloat16)
        grad_outer_matrix = jnp.einsum(
            "rth,rtd->hd", backward_third, branch_low, preferred_element_type=jnp.float32
        )
        grad_third = jnp.einsum(
            "rtd,hd->rth", branch_low, outer_low, preferred_element_type=jnp.float32
        )
        grad_normed = smooth_back(backward_normed_third, grad_third)
        grad_last_scale = jnp.sum(grad_normed * backward_scaled_third, axis=(0, 1))
        grad_last_shift = jnp.sum(grad_normed, axis=(0, 1))
        grad_mixed = back_shared(
            grad_normed, backward_scaled_third, backward_inverse_third, last_scale, inner
        )
        grad_conv_shift = jnp.sum(grad_mixed, axis=(0, 1))
        mixed_low = grad_mixed.astype(jnp.bfloat16)
        mixed_pad = widen(mixed_low, receptive_span)
        backward_masks = tap_masks(
            codes_local, codes_pad, tap_shifts, receptive_span, 1, kernel_taps
        )
        masks_back = tap_masks(codes_local, codes_pad, tap_shifts, receptive_span, -1, kernel_taps)
        backward_piece = lax.all_gather(backward_second_pad, "tensor", axis=2, tiled=True)
        parts = []
        for weight_tap_number in range(kernel_taps):
            weight_shifted = (
                lax.dynamic_slice_in_dim(
                    backward_piece, receptive_span + tap_shifts[weight_tap_number], length, 1
                )
                * backward_masks[weight_tap_number][..., None]
            )
            parts.append(
                jnp.einsum(
                    "rtc,rto->co", weight_shifted, mixed_low, preferred_element_type=jnp.float32
                )
            )
        grad_conv_matrix = jnp.stack(parts)
        terms = jnp.zeros((group, length, inner), jnp.float32)
        for backward_tap_number in range(kernel_taps):
            backward_shifted = (
                lax.dynamic_slice_in_dim(
                    mixed_pad, receptive_span - tap_shifts[backward_tap_number], length, 1
                )
                * masks_back[backward_tap_number][..., None]
            )
            terms = terms + jnp.einsum(
                "rto,co->rtc",
                backward_shifted,
                conv_low[backward_tap_number],
                preferred_element_type=jnp.float32,
            )
        grad_second = lax.psum_scatter(terms, "tensor", scatter_dimension=2, tiled=True)
        grad_normed = smooth_back(backward_normed_second, grad_second)
        grad_middle_scale = jnp.sum(grad_normed * backward_scaled_second, axis=(0, 1))
        grad_middle_shift = jnp.sum(grad_normed, axis=(0, 1))
        grad_hidden = back_shared(
            grad_normed, backward_scaled_second, backward_inverse_second, middle_scale, inner
        )
        grad_inner_shift = jnp.sum(grad_hidden, axis=(0, 1))
        hidden_low = grad_hidden.astype(jnp.bfloat16)
        grad_inner_matrix = jnp.einsum(
            "rtd,rth->dh", backward_first, hidden_low, preferred_element_type=jnp.float32
        )
        partial_in = jnp.einsum(
            "rth,dh->rtd", hidden_low, inner_low, preferred_element_type=jnp.float32
        )
        grad_first = lax.psum(partial_in, "tensor")
        grad_normed = smooth_back(backward_normed_first, grad_first)
        grad_first_scale = jnp.sum(grad_normed * backward_scaled_first, axis=(0, 1))
        grad_first_shift = jnp.sum(grad_normed, axis=(0, 1))
        grad_inputs = grad_out + back_whole(
            grad_normed, backward_scaled_first, backward_inverse_first, first_scale
        )
        grads = (
            grad_first_scale,
            grad_first_shift,
            grad_inner_matrix,
            grad_inner_shift,
            grad_middle_scale,
            grad_middle_shift,
            grad_conv_shift,
            grad_last_scale,
            grad_last_shift,
            grad_outer_matrix,
            grad_outer_shift,
        )
        grad_inputs, grads, grad_conv = (grad_inputs, grads, grad_conv_matrix)
        active = jnp.where(block_portion == 1, tick < MICRO, tick >= 1)
        totals = tuple(
            (jnp.where(active, total + grad, total) for total, grad in zip(totals, grads))
        )
        conv_total = jnp.where(active, conv_total + grad_conv, conv_total)
        grad_list.append(grad_inputs)
        if tick < MICRO:
            back_received = shifted_2(grad_inputs.astype(jnp.bfloat16), "pipe", -1).astype(
                grad_inputs.dtype
            )
    summed = jax.tree.map(lambda part: part.astype(jnp.float32), lax.psum(as_sent(totals), "seq"))
    encoder_part = jnp.where(block_portion == 0, conv_total, jnp.zeros_like(conv_total))
    decoder_part = jnp.where(
        block_portion == 1,
        conv_total[kernel_taps - dec_taps :],
        jnp.zeros_like(conv_total[kernel_taps - dec_taps :]),
    )
    conv_encoder_sum, conv_decoder_sum = (
        lax.psum(encoder_part.astype(jnp.bfloat16), ("pipe", "seq")).astype(jnp.float32),
        lax.psum(decoder_part.astype(jnp.bfloat16), ("pipe", "seq")).astype(jnp.float32),
    )
    section_output = jnp.where(
        block_portion == 0,
        jnp.concatenate(output_list[:MICRO], axis=0),
        jnp.concatenate(output_list[1:], axis=0),
    )[None]
    encoder_grads = jnp.concatenate([grad_list[MICRO - m] for m in range(MICRO)], axis=0)
    decoder_grads = jnp.concatenate([grad_list[MICRO - 1 - m] for m in range(MICRO)], axis=0)
    input_gradient = jnp.where(block_portion == 0, encoder_grads, decoder_grads)[None]
    stacked = tuple((item[None] for item in summed))
    return (
        (section_output, input_gradient)
        + stacked[:6]
        + (conv_encoder_sum, conv_decoder_sum)
        + stacked[6:]
    )


def solution(mesh):
    return jax.shard_map(
        on_device,
        mesh=mesh,
        in_specs=(
            P(None, "seq", None),
            P(None, "seq"),
            P(None, "seq"),
            P(None, "seq", None),
            P("pipe", None),
            P("pipe", None),
            P("pipe", None, "tensor"),
            P("pipe", "tensor"),
            P("pipe", "tensor"),
            P("pipe", "tensor"),
            P(None, None, "tensor"),
            P(None, None, "tensor"),
            P("pipe", "tensor"),
            P("pipe", "tensor"),
            P("pipe", "tensor"),
            P("pipe", "tensor", None),
            P("pipe", None),
        ),
        out_specs=(
            P("pipe", None, "seq", None),
            P("pipe", None, "seq", None),
            P("pipe", None),
            P("pipe", None),
            P("pipe", None, "tensor"),
            P("pipe", "tensor"),
            P("pipe", "tensor"),
            P("pipe", "tensor"),
            P(None, None, "tensor"),
            P(None, None, "tensor"),
            P("pipe", "tensor"),
            P("pipe", "tensor"),
            P("pipe", "tensor"),
            P("pipe", "tensor", None),
            P("pipe", None),
        ),
        check_vma=False,
    )
```

profile of v0, /device:TPU:1, one launch (start us, length us, event | category | flops | bytes accessed | tf_op | source)
XLA Modules:
  0.0 2635.8 jit_solution(3175702598461903317)
XLA Ops:
  54.2 29.6 %all_gather.10 = bf16[1,1088,400]{1,0,2:T(2,128)(2,1)S(1)} all-gather(bf16[1,1088,100]{1,0,2:T(2,128)(2,1)S(1)} %copy.56), channel_id=1, replica_groups=mesh['pipe'=2,'seq'=4,'tensor'=4] {'tensor'}, dimensions={2}, use_global_device_ids=true | all-gather | bytes 1088000 | tf_op jit(solution)/shard_map/all_gather | solution.py:198
  83.8 19.3 constant_dynamic-slice_fusion.66
  118.0 130.9 %all-reduce.47.cloned.1.call-done = f32[1,1024,800]{1,2,0:T(8,128)} async-done(((f32[1,1024,800]{1,2,0:T(8,128)}), f32[1,1024,800]{1,2,0:T(8,128)}) %all-reduce.47.cloned.1.call-update) | async-done | bytes 3276816 | tf_op jit(solution)/shard_map/psum | solution.py:232
  287.2 29.4 %all_gather.11 = bf16[1,1088,400]{1,0,2:T(2,128)(2,1)S(1)} all-gather(bf16[1,1088,100]{1,0,2:T(2,128)(2,1)S(1)} %copy.62), channel_id=1, replica_groups=mesh['pipe'=2,'seq'=4,'tensor'=4] {'tensor'}, dimensions={2}, use_global_device_ids=true | all-gather | bytes 1088000 | tf_op jit(solution)/shard_map/all_gather | solution.py:198
  351.6 129.8 %all-reduce.49.cloned.1.call-done = f32[1,1024,800]{1,2,0:T(8,128)} async-done(((f32[1,1024,800]{1,2,0:T(8,128)}), f32[1,1024,800]{1,2,0:T(8,128)}) %all-reduce.49.cloned.1.call-update) | async-done | bytes 3276816 | tf_op jit(solution)/shard_map/psum | solution.py:232
  518.8 29.4 %all_gather.12 = bf16[1,1088,400]{1,0,2:T(2,128)(2,1)S(1)} all-gather(bf16[1,1088,100]{1,0,2:T(2,128)(2,1)S(1)} %copy.68), channel_id=1, replica_groups=mesh['pipe'=2,'seq'=4,'tensor'=4] {'tensor'}, dimensions={2}, use_global_device_ids=true | all-gather | bytes 1088000 | tf_op jit(solution)/shard_map/all_gather | solution.py:198
  583.4 129.8 %all-reduce.51.cloned.1.call-done = f32[1,1024,800]{1,2,0:T(8,128)} async-done(((f32[1,1024,800]{1,2,0:T(8,128)}), f32[1,1024,800]{1,2,0:T(8,128)}) %all-reduce.51.cloned.1.call-update) | async-done | bytes 3276816 | tf_op jit(solution)/shard_map/psum | solution.py:232
  750.5 29.4 %all_gather.13 = bf16[1,1088,400]{1,0,2:T(2,128)(2,1)S(1)} all-gather(bf16[1,1088,100]{1,0,2:T(2,128)(2,1)S(1)} %copy.74), channel_id=1, replica_groups=mesh['pipe'=2,'seq'=4,'tensor'=4] {'tensor'}, dimensions={2}, use_global_device_ids=true | all-gather | bytes 1088000 | tf_op jit(solution)/shard_map/all_gather | solution.py:198
  815.2 129.8 %all-reduce.53.cloned.1.call-done = f32[1,1024,800]{1,2,0:T(8,128)} async-done(((f32[1,1024,800]{1,2,0:T(8,128)}), f32[1,1024,800]{1,2,0:T(8,128)}) %all-reduce.53.cloned.1.call-update) | async-done | bytes 3276816 | tf_op jit(solution)/shard_map/psum | solution.py:232
  983.6 29.7 %all_gather.14 = bf16[1,1088,400]{1,0,2:T(2,128)(2,1)S(1)} all-gather(bf16[1,1088,100]{1,0,2:T(2,128)(2,1)S(1)} %copy.80), channel_id=1, replica_groups=mesh['pipe'=2,'seq'=4,'tensor'=4] {'tensor'}, dimensions={2}, use_global_device_ids=true | all-gather | bytes 1088000 | tf_op jit(solution)/shard_map/all_gather | solution.py:198
  1013.3 19.4 constant_dynamic-slice_fusion.26
  1080.0 77.0 %all-reduce.63.cloned.1.call-done = f32[1,1024,400]{1,0,2:T(1,128)} async-done(((f32[1,1024,400]{1,0,2:T(1,128)}), f32[1,1024,400]{1,0,2:T(1,128)}) %all-reduce.63.cloned.1.call-update) | async-done | bytes 1638416
  1175.5 124.9 %all-reduce.55.cloned.1.call-done = f32[1,1024,800]{1,2,0:T(8,128)} async-done(((f32[1,1024,800]{1,2,0:T(8,128)}), f32[1,1024,800]{1,2,0:T(8,128)}) %all-reduce.55.cloned.1.call-update) | async-done | bytes 3276816 | tf_op jit(solution)/shard_map/psum | solution.py:340
  1349.7 71.7 %all-reduce.65.cloned.1.call-done = f32[1,1024,400]{1,0,2:T(1,128)} async-done(((f32[1,1024,400]{1,0,2:T(1,128)}), f32[1,1024,400]{1,0,2:T(1,128)}) %all-reduce.65.cloned.1.call-update) | async-done | bytes 1638416
  1439.4 125.3 %all-reduce.57.cloned.1.call-done = f32[1,1024,800]{1,2,0:T(8,128)} async-done(((f32[1,1024,800]{1,2,0:T(8,128)}), f32[1,1024,800]{1,2,0:T(8,128)}) %all-reduce.57.cloned.1.call-update) | async-done | bytes 3276816 | tf_op jit(solution)/shard_map/psum | solution.py:340
  1615.5 71.7 %all-reduce.67.cloned.1.call-done = f32[1,1024,400]{1,0,2:T(1,128)} async-done(((f32[1,1024,400]{1,0,2:T(1,128)}), f32[1,1024,400]{1,0,2:T(1,128)}) %all-reduce.67.cloned.1.call-update) | async-done | bytes 1638416
  1705.2 125.3 %all-reduce.59.cloned.1.call-done = f32[1,1024,800]{1,2,0:T(8,128)} async-done(((f32[1,1024,800]{1,2,0:T(8,128)}), f32[1,1024,800]{1,2,0:T(8,128)}) %all-reduce.59.cloned.1.call-update) | async-done | bytes 3276816 | tf_op jit(solution)/shard_map/psum | solution.py:340
  1896.5 58.6 %all-reduce.69.cloned.1.call-done = f32[1,1024,400]{1,0,2:T(1,128)} async-done(((f32[1,1024,400]{1,0,2:T(1,128)}), f32[1,1024,400]{1,0,2:T(1,128)}) %all-reduce.69.cloned.1.call-update) | async-done | bytes 1638416
  1990.8 107.7 %all-reduce.61.cloned.1.call-done = f32[1,1024,800]{1,2,0:T(8,128)} async-done(((f32[1,1024,800]{1,2,0:T(8,128)}), f32[1,1024,800]{1,2,0:T(8,128)}) %all-reduce.61.cloned.1.call-update) | async-done | bytes 3276816 | tf_op jit(solution)/shard_map/psum | solution.py:340
  2170.9 58.0 %all-reduce.71.cloned.1.call-done = f32[1,1024,400]{1,0,2:T(1,128)} async-done(((f32[1,1024,400]{1,0,2:T(1,128)}), f32[1,1024,400]{1,0,2:T(1,128)}) %all-reduce.71.cloned.1.call-update) | async-done | bytes 1638416
  2253.9 33.9 %all-reduce.75.cloned.1.call-done = (bf16[5,400,100]{2,1,0:T(8,128)(2,1)}, bf16[3,400,100]{2,1,0:T(8,128)(2,1)}) async-done(((bf16[5,400,100]{2,1,0:T(8,128)(2,1)}, bf16[3,400,100]{2,1,0:T(8,128)(2,1)}), (bf16[5,400,100]{2,1,0:T(8,128)(2,1)}, bf16[3,400,100]{2,1,0:T(8,128)(2,1)})) %all-reduce.75.cloned.1.call-update) | async-done | bytes 640016 | tf_op jit(solution)/shard_map/psum | solution.py:379
  2291.8 43.2 %all-reduce.77.cloned.1.call-done = (bf16[1,800,100]{1,2,0:T(8,128)(2,1)}, bf16[1,100,800]{2,1,0:T(8,128)(2,1)}) async-done(((bf16[1,800,100]{1,2,0:T(8,128)(2,1)}, bf16[1,100,800]{2,1,0:T(8,128)(2,1)}), (bf16[1,800,100]{1,2,0:T(8,128)(2,1)}, bf16[1,100,800]{2,1,0:T(8,128)(2,1)})) %all-reduce.77.cloned.1.call-update) | async-done | bytes 320016 | tf_op jit(solution)/shard_map/psum | solution.py:371
  2338.8 231.1 %all-reduce.73.cloned.1.call-done = (f32[1,1024,800]{1,2,0:T(8,128)}, f32[1,1024,800]{1,2,0:T(8,128)}) async-done(((f32[1,1024,800]{1,2,0:T(8,128)}, f32[1,1024,800]{1,2,0:T(8,128)}), (f32[1,1024,800]{1,2,0:T(8,128)}, f32[1,1024,800]{1,2,0:T(8,128)})) %all-reduce.73.cloned.1.call-update) | async-done | bytes 6553616 | tf_op jit(solution)/shard_map/psum | solution.py:232
  2605.5 23.3 maximum_select_fusion
  (1185 shorter events, 740.7 us)
Async XLA Ops:
  7.2 241.7 %all-reduce.47.cloned.1.call-start = ((), (), s32[]{:S(2)}) async-start(), calls=%async_computation | async-start | bytes 6553600 | tf_op jit(solution)/shard_map/psum | solution.py:232
  27.6 25.2 collective-permute-start
  30.8 22.1 collective-permute-start.1
  32.2 19.5 collective-permute-start.2
  36.1 15.5 collective-permute-start.3
  117.3 364.1 %all-reduce.49.cloned.1.call-start = ((), (), s32[]{:S(2)}) async-start(), calls=%async_computation.1 | async-start | bytes 6553600 | tf_op jit(solution)/shard_map/psum | solution.py:232
  252.3 7.7 collective-permute-start.4
  351.6 361.5 %all-reduce.51.cloned.1.call-start = ((), (), s32[]{:S(2)}) async-start(), calls=%async_computation.2 | async-start | bytes 6553600 | tf_op jit(solution)/shard_map/psum | solution.py:232
  583.3 361.6 %all-reduce.53.cloned.1.call-start = ((), (), s32[]{:S(2)}) async-start(), calls=%async_computation.3 | async-start | bytes 6553600 | tf_op jit(solution)/shard_map/psum | solution.py:232
  815.1 341.9 %all-reduce.63.cloned.1.call-start = ((), (), s32[]{:S(2)}) async-start(), calls=%async_computation.8 | async-start | bytes 3276800
  1057.6 10.7 collective-permute-start.16
  1060.6 8.4 collective-permute-start.17
  1078.7 221.7 %all-reduce.55.cloned.1.call-start = ((), (), s32[]{:S(2)}) async-start(), calls=%async_computation.4 | async-start | bytes 6553600 | tf_op jit(solution)/shard_map/psum | solution.py:340
  1175.0 246.3 %all-reduce.65.cloned.1.call-start = ((), (), s32[]{:S(2)}) async-start(), calls=%async_computation.9 | async-start | bytes 3276800
  1349.4 215.2 %all-reduce.57.cloned.1.call-start = ((), (), s32[]{:S(2)}) async-start(), calls=%async_computation.5 | async-start | bytes 6553600 | tf_op jit(solution)/shard_map/psum | solution.py:340
  1439.3 247.8 %all-reduce.67.cloned.1.call-start = ((), (), s32[]{:S(2)}) async-start(), calls=%async_computation.10 | async-start | bytes 3276800
  1615.2 215.4 %all-reduce.59.cloned.1.call-start = ((), (), s32[]{:S(2)}) async-start(), calls=%async_computation.6 | async-start | bytes 6553600 | tf_op jit(solution)/shard_map/psum | solution.py:340
  1705.2 249.9 %all-reduce.69.cloned.1.call-start = ((), (), s32[]{:S(2)}) async-start(), calls=%async_computation.11 | async-start | bytes 3276800
  1882.9 215.6 %all-reduce.61.cloned.1.call-start = ((), (), s32[]{:S(2)}) async-start(), calls=%async_computation.7 | async-start | bytes 6553600 | tf_op jit(solution)/shard_map/psum | solution.py:340
  1973.2 255.7 %all-reduce.71.cloned.1.call-start = ((), (), s32[]{:S(2)}) async-start(), calls=%async_computation.12 | async-start | bytes 3276800
  2112.2 11.8 collective-permute-start.27
  2157.6 130.2 %all-reduce.75.cloned.1.call-start = ((), (), s32[]{:S(2)}) async-start(), calls=%async_computation.14 | async-start | bytes 1638400 | tf_op jit(solution)/shard_map/psum | solution.py:379
  2170.8 164.2 %all-reduce.77.cloned.1.call-start = ((), (), s32[]{:S(2)}) async-start(), calls=%async_computation.15 | async-start | bytes 745472 | tf_op jit(solution)/shard_map/psum | solution.py:371
  2246.9 323.1 %all-reduce.73.cloned.1.call-start = ((), (), s32[]{:S(2)}) async-start(), calls=%async_computation.13 | async-start | bytes 13107200 | tf_op jit(solution)/shard_map/psum | solution.py:232
  (406 other events, 9271.6 us)
Sparse Core Ops, SparseCore 0:
  117.4 131.4 all-reduce.46
  351.7 129.6 all-reduce.48
  583.4 129.6 all-reduce.50
  815.2 129.6 all-reduce.52
  1078.9 78.1 all-reduce.62
  1175.1 125.2 all-reduce.54
  1349.5 71.7 all-reduce.64
  1439.4 125.2 all-reduce.56
  1615.3 71.7 all-reduce.66
  1705.3 125.2 all-reduce.58
  1883.0 72.0 all-reduce.68
  1973.3 125.2 all-reduce.60
  2157.7 71.0 all-reduce.70
  2232.9 54.7 all-reduce.74
  2290.9 43.9 all-reduce.76
  2337.8 232.1 all-reduce.72
where the time goes:
time: 2650 us; the launch traced here: 2640 us
  waiting for transfers between devices  1690 us (64%)
  blocking collectives  325 us (12%)
  other arithmetic  198 us (7%)
  local copies, waits for them, and re-layouts  165 us (6%)
  matrix products  144 us (5%)
  starting transfers between devices  73 us (3%)
  between operations  37 us (1%)
    psum x5, waiting for transfers between devices, forward(): product = lax.psum(partial_out, 'tensor')  751 us
    psum x4, waiting for transfers between devices, on_device(): grad_first = lax.psum(partial_in, 'tensor')  483 us
    unnamed x21, waiting for transfers between devices  337 us
    psum x20, blocking collectives, pair_sum(): return lax.psum((first, second), 'tensor')  165 us
    all_gather x5, blocking collectives, forward(): piece = lax.all_gather(second_pad, 'tensor', axis=2, tiled=True)  148 us
    dynamic_slice x5, local copies, waits for them, and re-layouts, forward(): lax.dynamic_slice_in_dim(piece, receptive_span + tap_shifts[tap_number],...  96.7 us
  transfers between devices with their start and end apart: 46, of which 29 were waited for; matrix products, arithmetic and copies ran while one was open for 3% of the time, Pallas kernels for 0%

commit v1 on v0

v1 whole, which is shorter than its diff:
```python
import functools
import math

import jax
import jax.numpy as jnp
from jax import lax
from jax.experimental import pallas as pl
from jax.experimental.pallas import tpu as pltpu
from jax.sharding import PartitionSpec as P

SPACING = 16
EPSILON = 1e-05
BF = jnp.bfloat16
F32 = jnp.float32
LANES = 512
ROOT = math.sqrt(2.0 / math.pi)
CUBIC = 0.044715
E_OFFSETS = tuple(SPACING * (k - 2) for k in range(5))
D_OFFSETS = (-2, -1, 0)
COLUMN = {-32: 0, -16: 1, 16: 2, 32: 3, -2: 4, -1: 5, 2: 6, 1: 7}
KEEP, OWN = 8, 9
TOK, MID, COT = 96, 64, 32


def dot(a, b):
    return lax.dot_general(a, b, (((1,), (0,)), ((), ())), preferred_element_type=F32)


def dot_nt(a, b):
    return lax.dot_general(a, b, (((1,), (1,)), ((), ())), preferred_element_type=F32)


def dot_tn(a, b):
    return lax.dot_general(a, b, (((0,), (0,)), ((), ())), preferred_element_type=F32)


def normalized(values, width):
    center = jnp.sum(values, axis=-1, keepdims=True) * (1.0 / width)
    square = jnp.sum(values * values, axis=-1, keepdims=True) * (1.0 / width)
    inverse = lax.rsqrt(square - center * center + EPSILON)
    return (values - center) * inverse, inverse


def gate(half):
    square = half * half
    return jnp.tanh(half * (2 * ROOT + (8 * CUBIC * ROOT) * square)), square


def slope(half, tanh, square):
    return (1.0 + tanh) * (0.5 + half * (1.0 - tanh) * (ROOT + (12 * CUBIC * ROOT) * square))


def activated(scaled, gain, bias):
    half = scaled * (0.5 * gain) + 0.5 * bias
    tanh, square = gate(half)
    return half + half * tanh, slope(half, tanh, square)


def back(weighted, scaled, inverse, width):
    first = jnp.sum(weighted, axis=-1, keepdims=True) * (1.0 / width)
    second = jnp.sum(weighted * scaled, axis=-1, keepdims=True) * (1.0 / width)
    return inverse * (weighted - first - scaled * second)


def rows8(values):
    count, width = values.shape
    return jnp.sum(values.reshape(count // 8, 8, width), axis=0)


def first_step():
    return (pl.program_id(0) == 0) & (pl.program_id(1) == 0)


def masked(values, mask_ref, offset):
    column = mask_ref[0, :, COLUMN[offset] : COLUMN[offset] + 1].astype(BF)
    return values * column


def middle(hidden, h_ref, row, inner, sec_ref, xh_ref, dg_ref, inv_ref):
    scaled, inverse = normalized(hidden, inner)
    value, grad = activated(scaled, h_ref[row : row + 1, :], h_ref[row + 1 : row + 2, :])
    if sec_ref is not None:
        sec_ref[0] = value.astype(BF)
    xh_ref[0] = scaled.astype(BF)
    dg_ref[0] = grad.astype(BF)
    inv_ref[0] = jnp.broadcast_to(inverse, inv_ref.shape[1:])
    return value.astype(BF)


def encoder_in(inner, meta, tok_ref, wi_ref, d_ref, h_ref, sec_ref, xh_ref, dg_ref, inv_ref):
    values = tok_ref[0]
    scaled, _ = normalized(values, values.shape[-1])
    half = scaled * (0.5 * d_ref[0:1, :]) + 0.5 * d_ref[1:2, :]
    tanh, _ = gate(half)
    first = (half + half * tanh).astype(BF)
    hidden = dot(first, wi_ref[...]) + h_ref[0:1, :]
    middle(hidden, h_ref, 1, inner, sec_ref, xh_ref, dg_ref, inv_ref)


def encoder_out(
    inner, chunk, meta, sec_ref, tok_ref, mask_ref, wc_ref, wo_ref, wi_ref, de_ref, he_ref, dd_ref, hd_ref,
    out_ref, xh3_ref, dg3_ref, inv3_ref, third_ref, sec2_ref, xh2_ref, dg2_ref, inv2_ref, keep_ref,
):
    start = pl.program_id(1) * chunk + (TOK - MID)
    total = None
    for k, offset in enumerate(E_OFFSETS):
        piece = sec_ref[0, pl.ds(pl.multiple_of(start + offset, 16), chunk), :]
        if offset:
            piece = masked(piece, mask_ref, offset)
        term = dot(piece, wc_ref[k])
        total = term if total is None else total + term
    mixed = total + he_ref[3:4, :]
    third = middle(mixed, he_ref, 4, inner, None, xh3_ref, dg3_ref, inv3_ref)
    keep_ref[...] = third
    third_ref[0] = keep_ref[:, pl.ds(pl.multiple_of(meta[1] * 128, 128), 128)]
    keep = mask_ref[0, :, KEEP : KEEP + 1]
    output = tok_ref[0] + keep * (dot(third, wo_ref[...]) + de_ref[2:3, :])
    out_ref[0] = output
    scaled, _ = normalized(output, output.shape[-1])
    half = scaled * (0.5 * dd_ref[0:1, :]) + 0.5 * dd_ref[1:2, :]
    tanh, _ = gate(half)
    first = (half + half * tanh).astype(BF)
    hidden = dot(first, wi_ref[...]) + hd_ref[0:1, :]
    middle(hidden, hd_ref, 1, inner, sec2_ref, xh2_ref, dg2_ref, inv2_ref)


def add_to(ref, value):
    ref[...] += value


def decoder_out(
    inner, chunk, length, meta, sec_ref, in_ref, cot_ref, mask_ref, wc_ref, wo_ref, dd_ref, hd_ref, final_ref,
    mine_ref, other_ref, mixed_ref, go_ref, gc_ref, gd_ref, gh_ref,
    third_ref, low_ref, mine_buf, other_buf, sems,
):
    del final_ref
    row, step = pl.program_id(0), pl.program_id(1)
    steps = pl.num_programs(1)

    @pl.when(first_step())
    def _():
        for ref in (go_ref, gc_ref, gd_ref, gh_ref):
            ref[...] = jnp.zeros_like(ref)

    start = pl.multiple_of(step * chunk + (MID - COT - 16), 16)
    window = sec_ref[0, pl.ds(start, chunk + 16), :].astype(F32)
    pieces = []
    total = None
    for k, offset in enumerate(D_OFFSETS):
        piece = window[16 + offset : 16 + offset + chunk].astype(BF)
        if offset:
            piece = masked(piece, mask_ref, offset)
        pieces.append(piece)
        term = dot(piece, wc_ref[k])
        total = term if total is None else total + term
    mixed = total + hd_ref[3:4, :]
    scaled, inverse = normalized(mixed, inner)
    value, grad = activated(scaled, hd_ref[4:5, :], hd_ref[5:6, :])
    third = value.astype(BF)
    keep = mask_ref[0, :, KEEP : KEEP + 1]
    own = mask_ref[0, :, OWN : OWN + 1]
    inputs = in_ref[0]
    output = inputs + keep * (dot(third, wo_ref[...]) + dd_ref[2:3, :])
    encoder_side = meta[0] == 0
    at = pl.ds(pl.multiple_of(step * chunk, 16), chunk)
    mine_buf[row, at, :] = jnp.where(encoder_side, inputs, output)
    other_buf[row, at, :] = jnp.where(encoder_side, output, inputs).astype(BF)

    branch = keep * cot_ref[0]
    branch_low = branch.astype(BF)
    gd_ref[0:8, :] += rows8(branch * own)
    grad_third = dot_nt(branch_low, wo_ref[...])
    grad_normed = grad * grad_third
    kept = grad_normed * own
    gh_ref[0:8, :] += rows8(kept * scaled)
    gh_ref[8:16, :] += rows8(kept)
    grad_mixed = back(grad_normed * hd_ref[4:5, :], scaled, inverse, inner)
    gh_ref[16:24, :] += rows8(grad_mixed * own)
    mixed_low = grad_mixed.astype(BF)
    mixed_ref[0] = mixed_low
    third_ref[...] = third
    low_ref[...] = mixed_low
    lanes = pl.ds(pl.multiple_of(meta[1] * 128, 128), 128)
    own_low = own.astype(BF)
    go_ref[...] += dot_tn(third_ref[:, lanes] * own_low, branch_low)
    mixed_own = low_ref[:, lanes] * own_low
    for k in range(3):
        gc_ref[k] += dot_tn(mixed_own, pieces[k])

    @pl.when(step == steps - 1)
    def _():
        target = meta[0] * pl.num_programs(0) + row
        pltpu.make_async_copy(mine_buf.at[row, COT : COT + length], mine_ref.at[target], sems.at[0, row]).start()
        pltpu.make_async_copy(other_buf.at[row, COT : COT + length], other_ref.at[row], sems.at[1, row]).start()

    @pl.when((step == steps - 1) & (row == pl.num_programs(0) - 1))
    def _():
        for r in range(mine_buf.shape[0]):
            target = meta[0] * pl.num_programs(0) + r
            pltpu.make_async_copy(mine_buf.at[r, COT : COT + length], mine_ref.at[target], sems.at[0, r]).wait()
            pltpu.make_async_copy(other_buf.at[r, COT : COT + length], other_ref.at[r], sems.at[1, r]).wait()


def inner_back(
    inner, grad_second, xh_ref, dg_ref, inv_ref, h_ref, wi_ref, inputs, d_ref, own, lanes, low_ref,
    gi_ref, gd_ref, gh_ref, base,
):
    scaled = xh_ref[0].astype(F32)
    inverse = inv_ref[0][:, 0:1]
    grad_normed = dg_ref[0].astype(F32) * grad_second
    kept = grad_normed if own is None else grad_normed * own
    gh_ref[base : base + 8, :] += rows8(kept * scaled)
    gh_ref[base + 8 : base + 16, :] += rows8(kept)
    grad_hidden = back(grad_normed * h_ref[1:2, :], scaled, inverse, inner)
    gh_ref[base + 16 : base + 24, :] += rows8(grad_hidden if own is None else grad_hidden * own)
    hidden_low = grad_hidden.astype(BF)
    low_ref[...] = hidden_low
    width = inputs.shape[-1]
    scaled1, inverse1 = normalized(inputs, width)
    value, grad = activated(scaled1, d_ref[0:1, :], d_ref[1:2, :])
    mine = low_ref[:, lanes]
    if own is not None:
        mine = mine * own.astype(BF)
    gi_ref[...] += dot_tn(mine, value.astype(BF))
    grad_normed1 = grad * dot_nt(hidden_low, wi_ref[...])
    kept = grad_normed1 if own is None else grad_normed1 * own
    gd_ref[0:8, :] += rows8(kept * scaled1)
    gd_ref[8:16, :] += rows8(kept)
    return back(grad_normed1 * d_ref[0:1, :], scaled1, inverse1, width)


def decoder_back(
    inner, chunk, meta, mixed_ref, xh2_ref, dg2_ref, inv2_ref, in_ref, cot_ref, mask_ref, wc_ref, wi_ref, dd_ref, hd_ref,
    xh3_ref, dg3_ref, inv3_ref, third_ref, wo_ref, he_ref,
    grad_ref, low3_ref, gi_ref, gd_ref, gh_ref, go_ref, gde_ref, ghe_ref,
    low_ref,
):
    @pl.when(first_step())
    def _():
        for ref in (gi_ref, gd_ref, gh_ref, go_ref, gde_ref, ghe_ref):
            ref[...] = jnp.zeros_like(ref)

    lanes = pl.ds(pl.multiple_of(meta[1] * 128, 128), 128)
    own = mask_ref[0, :, OWN : OWN + 1]
    start = pl.multiple_of(pl.program_id(1) * chunk, 16)
    window = mixed_ref[0, pl.ds(start, chunk + 16), :].astype(F32)
    total = None
    for k, offset in enumerate(D_OFFSETS):
        piece = window[-offset : chunk - offset].astype(BF)
        if offset:
            piece = masked(piece, mask_ref, -offset)
        term = dot_nt(piece, wc_ref[k])
        total = term if total is None else total + term
    grad_inputs = cot_ref[0] + inner_back(
        inner, total, xh2_ref, dg2_ref, inv2_ref, hd_ref, wi_ref, in_ref[0], dd_ref, own, lanes, low_ref,
        gi_ref, gd_ref, gh_ref, 0,
    )
    grad_ref[0] = grad_inputs
    branch = mask_ref[0, :, KEEP : KEEP + 1] * grad_inputs
    branch_low = branch.astype(BF)
    gde_ref[...] += rows8(branch * own)
    go_ref[...] += dot_tn(third_ref[0] * own.astype(BF), branch_low)
    scaled = xh3_ref[0].astype(F32)
    grad_normed = dg3_ref[0].astype(F32) * dot_nt(branch_low, wo_ref[...])
    kept = grad_normed * own
    ghe_ref[0:8, :] += rows8(kept * scaled)
    ghe_ref[8:16, :] += rows8(kept)
    grad_mixed = back(grad_normed * he_ref[4:5, :], scaled, inv3_ref[0][:, 0:1], inner)
    ghe_ref[16:24, :] += rows8(grad_mixed * own)
    low3_ref[0] = grad_mixed.astype(BF)


def encoder_back(
    inner, chunk, meta, mixed_ref, sec_ref, xh2_ref, dg2_ref, inv2_ref, in_ref, grad_ref, mask_ref, wc_ref, wi_ref, de_ref,
    he_ref, final_ref,
    mine_ref, other_ref, gi_ref, gc_ref, gd_ref, gh_ref,
    low_ref,
):
    del final_ref

    @pl.when(first_step())
    def _():
        for ref in (gi_ref, gc_ref, gd_ref, gh_ref):
            ref[...] = jnp.zeros_like(ref)

    lanes = pl.ds(pl.multiple_of(meta[1] * 128, 128), 128)
    step = pl.program_id(1)
    total = None
    for k, offset in enumerate(E_OFFSETS):
        piece = mixed_ref[0, pl.ds(pl.multiple_of(step * chunk + COT - offset, 16), chunk), :]
        if offset:
            piece = masked(piece, mask_ref, -offset)
        term = dot_nt(piece, wc_ref[k])
        total = term if total is None else total + term
    mixed_own = mixed_ref[0, pl.ds(pl.multiple_of(step * chunk + COT, 16), chunk), lanes]
    for k, offset in enumerate(E_OFFSETS):
        piece = sec_ref[0, pl.ds(pl.multiple_of(step * chunk + TOK + offset, 16), chunk), :]
        if offset:
            piece = masked(piece, mask_ref, offset)
        gc_ref[k] += dot_tn(mixed_own, piece)
    later = grad_ref[0]
    result = later + inner_back(
        inner, total, xh2_ref, dg2_ref, inv2_ref, he_ref, wi_ref, in_ref[0], de_ref, None, lanes, low_ref,
        gi_ref, gd_ref, gh_ref, 0,
    )
    encoder_side = meta[0] == 0
    mine_ref[0] = jnp.where(encoder_side, result, later)
    other_ref[0] = jnp.where(encoder_side, later, result).astype(BF)


def fill_rows(meta, recv_ref, final_ref, out_ref):
    del meta, final_ref
    out_ref[0] = recv_ref[0].astype(F32)


def call(body, meta, grid, ins, outs, scratch=(), aliases=None, name=None, flops=0, nbytes=0):
    args = [a for a, _ in ins]
    return pl.pallas_call(
        body,
        grid_spec=pltpu.PrefetchScalarGridSpec(
            num_scalar_prefetch=1,
            grid=grid,
            in_specs=[s for _, s in ins],
            out_specs=[s for _, s in outs],
            scratch_shapes=list(scratch),
        ),
        out_shape=[s for s, _ in outs],
        input_output_aliases=aliases or {},
        compiler_params=pltpu.CompilerParams(
            dimension_semantics=("arbitrary",) * len(grid), vmem_limit_bytes=58 * 1024 * 1024
        ),
        cost_estimate=pl.CostEstimate(flops=flops, bytes_accessed=nbytes, transcendentals=0),
        name=name,
    )(meta, *args)


def blocked(array, rows):
    return (array, pl.BlockSpec((1, rows, array.shape[2]), lambda r, i, m: (r, i, 0)))


def element(array, rows, base):
    return (
        array,
        pl.BlockSpec(
            (pl.Element(1), pl.Element(rows), pl.Element(array.shape[2])), lambda r, i, m: (r, pl.multiple_of(i * rows + base, 16), 0)
        ),
    )


def whole_row(array):
    return (array, pl.BlockSpec((1,) + array.shape[1:], lambda r, i, m: (r, 0, 0)))


def fixed(array):
    zeros = (0,) * array.ndim
    return (array, pl.BlockSpec(array.shape, lambda r, i, m: zeros))


def out_blocked(count, total, rows, width, dtype):
    return (
        jax.ShapeDtypeStruct((count, total, width), dtype),
        pl.BlockSpec((1, rows, width), lambda r, i, m: (r, i, 0)),
    )


def out_fixed(shape):
    zeros = (0,) * len(shape)
    return (jax.ShapeDtypeStruct(shape, F32), pl.BlockSpec(shape, lambda r, i, m: zeros))


def flip(x, axis, by):
    count = lax.axis_size(axis)
    return lax.ppermute(x, axis, [(i, i ^ by) for i in range(count)])


def gather(x, axis):
    me = lax.axis_index(axis)
    count = lax.axis_size(axis)
    result = jnp.zeros((count,) + x.shape, x.dtype)
    result = lax.dynamic_update_index_in_dim(result, x, me, 0)
    for by in range(1, count):
        result = lax.dynamic_update_index_in_dim(result, flip(x, axis, by), me ^ by, 0)
    return result


def sum_over(x, axis):
    count = lax.axis_size(axis)
    me = lax.axis_index(axis)
    parts = x.reshape((count, x.shape[0] // count) + x.shape[1:])
    low = parts.astype(BF)
    total = lax.dynamic_index_in_dim(parts, me, 0, keepdims=False)
    for by in range(1, count):
        total = total + flip(lax.dynamic_index_in_dim(low, me ^ by, 0, keepdims=False), axis, by).astype(F32)
    return gather(total.astype(BF), axis).astype(F32).reshape(x.shape)


def pad_to(x, axis, size):
    widths = [(0, 0)] * x.ndim
    widths[axis] = (0, size - x.shape[axis])
    return jnp.pad(x, widths)


def on_device(
    tokens, segments, pad_mask, cotangent, gain_first, bias_first, weight_inner, bias_inner, gain_middle, bias_middle,
    weight_conv_encoder, weight_conv_decoder, bias_conv, gain_last, bias_last, weight_outer, bias_outer,
):
    pipe, seq, tensor = (lax.axis_index(a) for a in ("pipe", "seq", "tensor"))
    n_pipe, n_seq, n_tensor = (lax.axis_size(a) for a in ("pipe", "seq", "tensor"))
    rows_all, length, width = tokens.shape
    rows = rows_all // n_pipe
    local = weight_conv_encoder.shape[2]
    inner = weight_conv_encoder.shape[1]
    lanes = LANES // n_tensor
    encoder_side = pipe == 0
    meta = jnp.stack([pipe, tensor * lanes // 128]).astype(jnp.int32)

    def mine_rows(array):
        return lax.dynamic_slice_in_dim(array, pipe * rows, rows, 0)

    def quarter(array, axis):
        size = array.shape[axis] // n_seq
        return lax.dynamic_slice_in_dim(array, seq * size, size, axis)

    small = jnp.stack([bias_inner[0], gain_middle[0], bias_middle[0], bias_conv[0], gain_last[0], bias_last[0]])
    small = gather(pad_to(pad_to(small, 1, lanes), 0, 8), "tensor")
    small = jnp.transpose(small, (1, 0, 2)).reshape(8, LANES)
    large = pad_to(jnp.stack([gain_first[0], bias_first[0], bias_outer[0]]), 0, 8)
    small2, large2 = flip(small, "pipe", 1), flip(large, "pipe", 1)
    he, hd = jnp.where(encoder_side, small, small2), jnp.where(encoder_side, small2, small)
    de, dd = jnp.where(encoder_side, large, large2), jnp.where(encoder_side, large2, large)

    def both(full):
        other = flip(full, "pipe", 1)
        return jnp.where(encoder_side, full, other), jnp.where(encoder_side, other, full)

    in_piece = pad_to(quarter(weight_inner[0].astype(BF), 0), 1, lanes)
    in_all = gather(gather(in_piece, "tensor"), "seq")
    in_full = jnp.transpose(in_all, (0, 2, 1, 3)).reshape(width, LANES)
    inner_e, inner_d = both(in_full)

    conv_mine = jnp.where(
        encoder_side,
        weight_conv_encoder[:4],
        jnp.concatenate([weight_conv_encoder[4:], weight_conv_decoder], axis=0),
    ).astype(BF)
    conv_mine = pad_to(conv_mine.reshape(4, n_tensor, local, local), 3, lanes)
    conv_mine = pad_to(conv_mine, 2, lanes).reshape(4, LANES, lanes)
    conv_all = gather(gather(quarter(conv_mine, 1), "tensor"), "seq")
    conv_full = jnp.transpose(conv_all, (2, 0, 3, 1, 4)).reshape(4, LANES, LANES)
    conv_a, conv_b = both(conv_full)
    conv_e = jnp.concatenate([conv_a, conv_b[:1]], axis=0)
    conv_d = conv_b[1:]

    out_piece = quarter(pad_to(weight_outer[0].astype(BF), 0, lanes), 0)
    out_all = gather(gather(out_piece, "tensor"), "seq")
    out_full = jnp.transpose(out_all, (1, 0, 2, 3)).reshape(LANES, width)
    outer_e, outer_d = both(out_full)

    def neighbours(array, reach):
        right = [(i, i + 1) for i in range(n_seq - 1)]
        left = [(i + 1, i) for i in range(n_seq - 1)]
        before = lax.ppermute(array[:, length - reach :], "seq", right)
        after = lax.ppermute(array[:, :reach], "seq", left)
        return before, after

    tokens_mine, cotangent_mine = mine_rows(tokens), mine_rows(cotangent)
    before, after = neighbours(tokens_mine.astype(BF), 80)
    ends = jnp.zeros((rows, TOK - 80, width), F32)
    tok_ext = jnp.concatenate([ends, before.astype(F32), tokens_mine, after.astype(F32), ends], axis=1)
    before, after = neighbours(cotangent_mine.astype(BF), 48)
    cot_ext = jnp.concatenate(
        [before[:, 48 - COT :].astype(F32), cotangent_mine, after.astype(F32)], axis=1
    )
    codes = mine_rows(jnp.where(pad_mask == 1, segments + 1, 0)) + 1
    before, after = neighbours(codes, 128)
    codes = jnp.concatenate([before, codes, after], axis=1) - 1
    total = length + 2 * TOK
    here = codes[:, 128 - TOK : 128 - TOK + total]
    columns = [None] * 16
    for offset, index in COLUMN.items():
        there = codes[:, 128 - TOK + offset : 128 - TOK + offset + total]
        columns[index] = (there == here).astype(F32)
    columns[KEEP] = (here > 0).astype(F32)
    place = jnp.arange(total)
    columns[OWN] = jnp.broadcast_to(((place >= TOK) & (place < TOK + length)).astype(F32), here.shape)
    for index in range(10, 16):
        columns[index] = jnp.zeros_like(columns[0])
    masks = jnp.stack(columns, axis=-1)

    n1, n2, n3, n4, n5 = 4, 4, 3, 4, 4
    c1, c2, c3 = total // n1, (length + 2 * MID) // n2, (length + 80) // n3
    c4, c5 = (length + 2 * COT) // n4, length // n5
    sec_e, xh2_e, dg2_e, inv2_e = call(
        functools.partial(encoder_in, inner),
        meta,
        (rows, n1),
        [blocked(tok_ext, c1), fixed(inner_e), fixed(de), fixed(he)],
        [out_blocked(rows, total, c1, LANES, BF)] * 3 + [out_blocked(rows, total, c1, 128, F32)],
        name="encoder_in",
        flops=2 * rows * total * width * LANES,
    )
    t2 = length + 2 * MID
    out_e, xh3_e, dg3_e, inv3_e, third_e, sec_d, xh2_d, dg2_d, inv2_d = call(
        functools.partial(encoder_out, inner, c2),
        meta,
        (rows, n2),
        [
            whole_row(sec_e), element(tok_ext, c2, TOK - MID), element(masks, c2, TOK - MID),
            fixed(conv_e), fixed(outer_e), fixed(inner_d), fixed(de), fixed(he), fixed(dd), fixed(hd),
        ],
        [
            out_blocked(rows, t2, c2, width, F32),
            out_blocked(rows, t2, c2, LANES, BF), out_blocked(rows, t2, c2, LANES, BF), out_blocked(rows, t2, c2, 128, F32),
            out_blocked(rows, t2, c2, 128, BF),
            out_blocked(rows, t2, c2, LANES, BF), out_blocked(rows, t2, c2, LANES, BF),
            out_blocked(rows, t2, c2, LANES, BF), out_blocked(rows, t2, c2, 128, F32),
        ],
        [pltpu.VMEM((c2, LANES), BF)],
        name="encoder_out",
        flops=2 * rows * t2 * LANES * (5 * LANES + 2 * width),
    )
    t3 = length + 80
    final = jax.ShapeDtypeStruct((rows_all, length, width), F32)
    hbm = pl.BlockSpec(memory_space=pl.ANY)
    seed = jnp.zeros((8, 128), F32)
    mine_out, other_out, mixed_d, go_d, gc_d, gdo_d, gh3_d = call(
        functools.partial(decoder_out, inner, c3, length),
        meta,
        (rows, n3),
        [
            whole_row(sec_d), element(out_e, c3, MID - COT), blocked(cot_ext, c3), element(masks, c3, TOK - COT),
            fixed(conv_d), fixed(outer_d), fixed(dd), fixed(hd), (seed, hbm),
        ],
        [
            (final, hbm),
            (jax.ShapeDtypeStruct((rows, length, width), BF), hbm),
            out_blocked(rows, t3, c3, LANES, BF),
            out_fixed((128, width)), out_fixed((3, 128, LANES)), out_fixed((8, width)), out_fixed((24, LANES)),
        ],
        [
            pltpu.VMEM((c3, LANES), BF), pltpu.VMEM((c3, LANES), BF),
            pltpu.VMEM((rows, t3, width), F32), pltpu.VMEM((rows, t3, width), BF),
            pltpu.SemaphoreType.DMA((2, rows)),
        ],
        name="decoder_out",
        flops=2 * rows * t3 * LANES * (3 * LANES + 2 * width + 3 * 128),
    )
    t4 = length + 2 * COT
    grad_d, mixed_e, gi_d, gd_d, gh2_d, go_e, gdo_e, gh3_e = call(
        functools.partial(decoder_back, inner, c4),
        meta,
        (rows, n4),
        [
            whole_row(mixed_d), element(xh2_d, c4, MID - COT), element(dg2_d, c4, MID - COT), element(inv2_d, c4, MID - COT),
            element(out_e, c4, MID - COT), blocked(cot_ext, c4), element(masks, c4, TOK - COT),
            fixed(conv_d), fixed(inner_d), fixed(dd), fixed(hd),
            element(xh3_e, c4, MID - COT), element(dg3_e, c4, MID - COT), element(inv3_e, c4, MID - COT),
            element(third_e, c4, MID - COT), fixed(outer_e), fixed(he),
        ],
        [
            out_blocked(rows, t4, c4, width, F32), out_blocked(rows, t4, c4, LANES, BF),
            out_fixed((128, width)), out_fixed((16, width)), out_fixed((24, LANES)),
            out_fixed((128, width)), out_fixed((8, width)), out_fixed((24, LANES)),
        ],
        [pltpu.VMEM((c4, LANES), BF)],
        name="decoder_back",
        flops=2 * rows * t4 * LANES * (3 * LANES + 3 * width),
    )
    mine_grad, other_grad, gi_e, gc_e, gd_e, gh2_e = call(
        functools.partial(encoder_back, inner, c5),
        meta,
        (rows, n5),
        [
            whole_row(mixed_e), whole_row(sec_e),
            element(xh2_e, c5, TOK), element(dg2_e, c5, TOK), element(inv2_e, c5, TOK),
            element(tok_ext, c5, TOK), element(grad_d, c5, COT), element(masks, c5, TOK),
            fixed(conv_e), fixed(inner_e), fixed(de), fixed(he), (seed, hbm),
        ],
        [
            (final, pl.BlockSpec((1, c5, width), lambda r, i, m: (m[0] * rows + r, i, 0))),
            out_blocked(rows, length, c5, width, BF),
            out_fixed((128, width)), out_fixed((5, 128, LANES)), out_fixed((16, width)), out_fixed((24, LANES)),
        ],
        [pltpu.VMEM((c5, LANES), BF)],
        name="encoder_back",
        flops=2 * rows * length * LANES * (5 * LANES + 2 * width + 5 * 128),
    )

    def finish(mine, other):
        return call(
            fill_rows,
            meta,
            (rows, 4),
            [blocked(flip(other, "pipe", 1), length // 4), (mine, hbm)],
            [
                (
                    final,
                    pl.BlockSpec((1, length // 4, width), lambda r, i, m: ((1 - m[0]) * rows + r, i, 0)),
                )
            ],
            aliases={2: 0},
            name="fill_rows",
            nbytes=rows * length * width * 6,
        )[0]

    section_output = finish(mine_out, other_out)[None]
    input_gradient = finish(mine_grad, other_grad)[None]

    def pick(e, d):
        kept = jnp.where(encoder_side, e, d)
        sent = jnp.where(encoder_side, d, e)
        return kept + flip(sent.astype(BF), "pipe", 1).astype(F32)

    offset = (tensor * lanes) % 128

    def own(array):
        return lax.dynamic_slice_in_dim(array, offset, lanes, array.ndim - 2)

    inner_sum, outer_sum = pick(own(gi_e), own(gi_d)), pick(own(go_e), own(go_d))
    conv_sum = pick(own(gc_e[:4]), own(jnp.concatenate([gc_e[4:], gc_d], axis=0)))
    sizes = [inner_sum.size, outer_sum.size, conv_sum.size]
    flat = jnp.concatenate([inner_sum.reshape(-1), outer_sum.reshape(-1), conv_sum.reshape(-1)])
    unit = 128 * 16 * n_seq
    flat = pad_to(flat, 0, -(-flat.size // unit) * unit).reshape(-1, 128)
    flat = sum_over(flat, "seq").reshape(-1)
    grad_inner = jnp.transpose(flat[: sizes[0]].reshape(lanes, width)[:local])
    grad_outer = flat[sizes[0] : sizes[0] + sizes[1]].reshape(lanes, width)[:local]
    conv_sum = flat[sizes[0] + sizes[1] : sum(sizes)].reshape(4, lanes, n_tensor, lanes)
    conv_sum = conv_sum[:, :local, :, :local].reshape(4, local, inner)
    conv_sum = jnp.transpose(conv_sum, (0, 2, 1))
    conv_other = flip(conv_sum.astype(BF), "pipe", 1).astype(F32)
    conv_first = jnp.where(encoder_side, conv_sum, conv_other)
    conv_second = jnp.where(encoder_side, conv_other, conv_sum)
    grad_conv_e = jnp.concatenate([conv_first, conv_second[:1]], axis=0)
    grad_conv_d = conv_second[1:]

    def fold(array, count):
        return jnp.sum(array.reshape(count, 8, array.shape[-1]), axis=1)

    wide = pick(
        jnp.concatenate([fold(gd_e, 2), fold(gdo_e, 1)], axis=0), jnp.concatenate([fold(gd_d, 2), fold(gdo_d, 1)], axis=0)
    )
    narrow = pick(
        jnp.concatenate([fold(gh2_e, 3), fold(gh3_e, 3)], axis=0), jnp.concatenate([fold(gh2_d, 3), fold(gh3_d, 3)], axis=0)
    )
    narrow = lax.dynamic_slice_in_dim(narrow, tensor * lanes, lanes, 1)
    vectors = jnp.concatenate([wide.reshape(-1), narrow.reshape(-1)])
    count = vectors.size
    vectors = pad_to(vectors, 0, -(-count // unit) * unit).reshape(-1, 128)
    vectors = sum_over(vectors, "seq").reshape(-1)
    wide = vectors[: 3 * width].reshape(3, width)
    narrow = vectors[3 * width : count].reshape(6, lanes)[:, :local]

    return (
        section_output,
        input_gradient,
        wide[0][None],
        wide[1][None],
        grad_inner[None],
        narrow[2][None],
        narrow[0][None],
        narrow[1][None],
        grad_conv_e,
        grad_conv_d,
        narrow[5][None],
        narrow[3][None],
        narrow[4][None],
        grad_outer[None],
        wide[2][None],
    )


def solution(mesh):
    return jax.shard_map(
        on_device,
        mesh=mesh,
        in_specs=(
            P(None, "seq", None),
            P(None, "seq"),
            P(None, "seq"),
            P(None, "seq", None),
            P("pipe", None),
            P("pipe", None),
            P("pipe", None, "tensor"),
            P("pipe", "tensor"),
            P("pipe", "tensor"),
            P("pipe", "tensor"),
            P(None, None, "tensor"),
            P(None, None, "tensor"),
            P("pipe", "tensor"),
            P("pipe", "tensor"),
            P("pipe", "tensor"),
            P("pipe", "tensor", None),
            P("pipe", None),
        ),
        out_specs=(
            P("pipe", None, "seq", None),
            P("pipe", None, "seq", None),
            P("pipe", None),
            P("pipe", None),
            P("pipe", None, "tensor"),
            P("pipe", "tensor"),
            P("pipe", "tensor"),
            P("pipe", "tensor"),
            P(None, None, "tensor"),
            P(None, None, "tensor"),
            P("pipe", "tensor"),
            P("pipe", "tensor"),
            P("pipe", "tensor"),
            P("pipe", "tensor", None),
            P("pipe", None),
        ),
        check_vma=False,
    )
```

time: 2650 us -> 522 us (0.20)
  waiting for transfers between devices: 1690 us -> 38 us
  blocking collectives: 325 us -> 0 us
  other arithmetic: 198 us -> 42.8 us
  Pallas kernels: 0 us -> 152 us
  matrix products: 144 us -> 0 us
  between operations: 37 us -> 1.91 us
  local copies, waits for them, and re-layouts: 165 us -> 194 us
    psum x11 -> x0, waiting for transfers between devices: 1310 us -> none  [the longest x5 751 us: forward(): product = lax.psum(partial_out, 'tensor')]
    unnamed x21 -> x0, waiting for transfers between devices: 337 us -> none
    psum x21 -> x0, blocking collectives: 178 us -> none  [the longest x20 165 us: pair_sum(): return lax.psum((first, second), 'tensor')]
    pallas_call x0 -> x7, Pallas kernels: none -> 152 us  [call(): pl.pallas_call(body, grid_spec=pltpu.PrefetchScalarGridSpec(num_scalar_pr...]
    all_gather x5 -> x0, blocking collectives: 148 us -> none  [forward(): piece = lax.all_gather(second_pad, 'tensor', axis=2, tiled=True)]
    dot_general x105 -> x0, matrix products: 144 us -> none  [the longest x25 36.7 us: on_device(): jnp.einsum('rtc,rto->co', weight_shifted, mixed_low, preferred_element_ty...]
    dynamic_slice x5 -> x4, local copies, waits for them, and re-layouts: 96.7 us -> 13.3 us  [the longest x1 12.3 us: mine_rows(): return lax.dynamic_slice_in_dim(array, pipe * rows, rows, 0)]
    reduce_sum x22 -> x8, other arithmetic: 78.7 us -> 1.8 us  [fold(): return jnp.sum(array.reshape(count, 8, array.shape[-1]), axis=1)]
  transfers between devices with their start and end apart: 46 -> 52, of which waited for: 29 -> 12; matrix products, arithmetic and copies ran while one was open for 3% -> 40% of each run, Pallas kernels for 0% -> 4%
where the time goes in v1:
time: 522 us; the launch traced here: 513 us
  local copies, waits for them, and re-layouts  194 us (37%)
  Pallas kernels  152 us (29%)
  starting transfers between devices  84.5 us (16%)
  other arithmetic  42.8 us (8%)
  waiting for transfers between devices  38 us (7%)
    pallas_call x7, Pallas kernels, call(): pl.pallas_call(body, grid_spec=pltpu.PrefetchScalarGridSpec(num_scalar_pr...  152 us
    ppermute x46, starting transfers between devices, flip(): return lax.ppermute(x, axis, [(i, i ^ by) for i in range(count)])  67 us
    unnamed x64, local copies, waits for them, and re-layouts  56.5 us
    dynamic_update_slice x27, local copies, waits for them, and re-layouts, gather(): lax.dynamic_update_index_in_dim(result, flip(x, axis, by), me ^ by, 0)  38.6 us
    ppermute x46, waiting for transfers between devices, flip(): return lax.ppermute(x, axis, [(i, i ^ by) for i in range(count)])  38 us
    another operation x13, local copies, waits for them, and re-layouts, on_device(): masks = jnp.stack(columns, axis=-1)  24.1 us
    dynamic_update_slice x7, local copies, waits for them, and re-layouts, gather(): result = lax.dynamic_update_index_in_dim(result, x, me, 0)  14.2 us
    ppermute x3, starting transfers between devices, neighbours(): before = lax.ppermute(array[:, length - reach:], 'seq', right)  13.6 us
  transfers between devices with their start and end apart: 52, of which 12 were waited for; matrix products, arithmetic and copies ran while one was open for 40% of the time, Pallas kernels for 4%

profile of v1, /device:TPU:1, one launch (start us, length us, event | category | flops | bytes accessed | tf_op | source)
XLA Modules:
  0.0 513.2 jit_solution(16598793783645948545)
XLA Ops:
  15.7 12.3 %constant_dynamic-slice_fusion.7 = (f32[2,1024,800]{1,2,0:T(8,128)}, f32[2,1024,800]{1,2,0:T(8,128)}) fusion(f32[4,1024,800]{1,2,0:T(8,128)} %param.20, s32[]{:T(128)S(6)} %select_n.242, f32[4,1024,800]{1,2,0:T(8,128)} %param.17), kind=kLoop, calls=%fused_computation.106 | loop fusion | bytes 26214404 | tf_op jit(solution)/shard_map/dynamic_slice | solution.py:418
  28.0 7.9 %copy.425 = f32[2,1024,800]{2,1,0:T(8,128)} copy(f32[2,1024,800]{1,2,0:T(8,128)} %get-tuple-element.331) | data formatting | bytes 13107200
  40.5 7.9 %copy.426 = f32[2,1024,800]{2,1,0:T(8,128)} copy(f32[2,1024,800]{1,2,0:T(8,128)} %get-tuple-element.330) | data formatting | bytes 13107200
  56.0 7.6 %dynamic_update_slice.129 = bf16[4,4,128,128]{3,0,2,1:T(4,128)(2,1)} dynamic-update-slice(bf16[4,4,128,128]{3,0,2,1:T(4,128)(2,1)} %broadcast_in_dim.184, bf16[1,4,128,128]{3,0,2,1:T(2,128)(2,1)S(1)} %copy.402, s32[]{:T(128)S(6)} %select_n.245, s32[]{:T(128)} %constant.177.clone.1, s32[]{:T(128)} %constant.177.clone.1, s32[]{:T(128)} %constant.177.clone.1) | dynamic-update-slice | bytes 262148 | tf_op jit(solution)/shard_map/jit(dynamic_update_index_in_dim)/dynamic_update_slice | solution.py:380
  93.2 9.4 %stack.103.mask_ref = f32[2,1216,16]{2,1,0:T(8,128)} concatenate(f32[2,1216,1]{2,1,0:T(8,128)S(1)} %copy.393, f32[2,1216,1]{2,1,0:T(8,128)S(1)} %copy.394, f32[2,1216,1]{2,1,0:T(8,128)} %copy.395, f32[2,1216,1]{2,1,0:T(8,128)} %copy.396, f32[2,1216,1]{2,1,0:T(8,128)} %copy.397, f32[2,1216,1]{2,1,0:T(8,128)} %copy.398, f32[2,1216,1]{2,1,0:T(8,128)} %copy.399, ...), dimensions={2} | concatenate | bytes 311296 | tf_op jit(solution)/shard_map/stack | solution.py:488
  142.1 7.6 %dynamic_update_slice.130 = bf16[4,4,128,128]{3,0,2,1:T(4,128)(2,1)} dynamic-update-slice(bf16[4,4,128,128]{3,0,2,1:T(4,128)(2,1)} %dynamic_update_slice.129, bf16[1,4,128,128]{3,0,2,1:T(2,128)(2,1)S(1)} %copy.403, s32[]{:T(128)S(6)} %select_n.246, s32[]{:T(128)} %constant.177.clone.1, s32[]{:T(128)} %constant.177.clone.1, s32[]{:T(128)} %constant.177.clone.1) | dynamic-update-slice | bytes 262148 | tf_op jit(solution)/shard_map/jit(dynamic_update_index_in_dim)/dynamic_update_slice | solution.py:382
  149.7 7.6 %dynamic_update_slice.131 = bf16[4,4,128,128]{3,0,2,1:T(4,128)(2,1)} dynamic-update-slice(bf16[4,4,128,128]{3,0,2,1:T(4,128)(2,1)} %dynamic_update_slice.130, bf16[1,4,128,128]{3,0,2,1:T(2,128)(2,1)S(1)} %copy.404, s32[]{:T(128)S(6)} %select_n.247, s32[]{:T(128)} %constant.177.clone.1, s32[]{:T(128)} %constant.177.clone.1, s32[]{:T(128)} %constant.177.clone.1) | dynamic-update-slice | bytes 262148 | tf_op jit(solution)/shard_map/jit(dynamic_update_index_in_dim)/dynamic_update_slice | solution.py:382
  157.3 7.6 %dynamic_update_slice.132 = bf16[4,4,128,128]{3,0,2,1:T(4,128)(2,1)} dynamic-update-slice(bf16[4,4,128,128]{3,0,2,1:T(4,128)(2,1)} %dynamic_update_slice.131, bf16[1,4,128,128]{3,0,2,1:T(2,128)(2,1)S(1)} %copy.405, s32[]{:T(128)S(6)} %select_n.248, s32[]{:T(128)} %constant.177.clone.1, s32[]{:T(128)} %constant.177.clone.1, s32[]{:T(128)} %constant.177.clone.1) | dynamic-update-slice | bytes 262148 | tf_op jit(solution)/shard_map/jit(dynamic_update_index_in_dim)/dynamic_update_slice | solution.py:382
  196.9 6.0 %collective-permute-done.21 = bf16[4,4,128,128]{3,0,2,1:T(4,128)(2,1)S(1)} collective-permute-done((bf16[4,4,128,128]{3,0,2,1:T(4,128)(2,1)}, bf16[4,4,128,128]{3,0,2,1:T(4,128)(2,1)S(1)}, u32[]{:S(2)}, u32[]{:S(2)}) %collective-permute-start.21) | collective-permute-done | bytes 524320 | tf_op jit(solution)/shard_map/ppermute | solution.py:373
  202.9 11.6 %collective-permute-start.8 = (bf16[800,512]{1,0:T(8,128)(2,1)}, bf16[800,512]{1,0:T(8,128)(2,1)}, u32[]{:S(2)}, u32[]{:S(2)}) collective-permute-start(bf16[800,512]{1,0:T(8,128)(2,1)} %bitcast.188), channel_id=1, source_target_pairs={{0,16},{16,0},{1,17},{17,1},{2,18},{18,2},{3,19},{19,3},{4,20},{20... | collective-permute-start | bytes 2457608 | tf_op jit(solution)/shard_map/ppermute | solution.py:373
  223.3 6.6 %constant_dynamic-update-slice_fusion.8 = f32[2,1216,800]{2,1,0:T(8,128)} fusion(f32[2,1216,800]{2,1,0:T(8,128)} %convert_dynamic-update-slice_fusion.1, f32[2,1024,800]{2,1,0:T(8,128)} %copy.425), kind=kLoop, calls=%fused_computation.114 | loop fusion | bytes 14680064
  235.7 14.3 %encoder_in.1 = (bf16[2,1216,512]{2,1,0:T(8,128)(2,1)}, bf16[2,1216,512]{2,1,0:T(8,128)(2,1)}, bf16[2,1216,512]{2,1,0:T(8,128)(2,1)}, f32[2,1216,128]{2,1,0:T(8,128)}) custom-call(s32[2]{0:T(128)} %pad_add_fusion.meta, f32[2,1216,800]{2,1,0:T(8,128)} %broadcast_dynamic-update-slice_fusion.1.tok_ref.in_ref, bf16[800,512]{1,0:T(8,128)(2,1)} %get-tuple-element.293.wi_ref, ...), custom_call_target="tpu_custom_call" | custom-call | flops 1992294400 | tf_op jit(solution)/shard_map/encoder_in/pallas_call | solution.py:318
  257.3 27.9 %encoder_out.1 = (f32[2,1152,800]{2,1,0:T(8,128)}, bf16[2,1152,512]{2,1,0:T(8,128)(2,1)}, bf16[2,1152,512]{2,1,0:T(8,128)(2,1)}, f32[2,1152,128]{2,1,0:T(8,128)}...) custom-call(s32[2]{0:T(128)} %pad_add_fusion.meta, ...), custom_call_target="tpu_custom_call" | custom-call | flops 9814671360 | tf_op jit(solution)/shard_map/encoder_out/pallas_call | solution.py:318
  285.9 33.6 %decoder_out.1 = (f32[4,1024,800]{2,1,0:T(8,128)}, bf16[2,1024,800]{2,1,0:T(8,128)(2,1)}, bf16[2,1104,512]{2,1,0:T(8,128)(2,1)}, f32[128,800]{1,0:T(8,128)}, f32...) custom-call(s32[2]{0:T(128)} %pad_add_fusion.meta, bf16[2,1152,512]{2,1,0:T(8,128)(2,1)} %get-tuple-element.50.sec_ref, ...), custom_call_target="tpu_custom_call" | custom-call | flops 7958691840 | tf_op jit(solution)/shard_map/decoder_out/pallas_call | solution.py:318
  319.5 33.3 %decoder_back.1 = (f32[2,1088,800]{2,1,0:T(8,128)}, bf16[2,1088,512]{2,1,0:T(8,128)(2,1)}, f32[128,800]{1,0:T(8,128)}, f32[16,800]{1,0:T(8,128)}, f32[24,512]{1,...) custom-call(s32[2]{0:T(128)} %pad_add_fusion.meta, ...), custom_call_target="tpu_custom_call" | custom-call | flops 8770289664 | tf_op jit(solution)/shard_map/decoder_back/pallas_call | solution.py:318
  352.9 27.1 %encoder_back.1 = (f32[4,1024,800]{2,1,0:T(8,128)}, bf16[2,1024,800]{2,1,0:T(8,128)(2,1)}, f32[128,800]{1,0:T(8,128)}, f32[5,128,512]{2,1,0:T(8,128)}, f32[16,800]{1,0:T(8,128)}, /*index=5*/f32[24,512]{1,0:T(8,128)}) custom-call(s32[2]{0:T(128)} %pad_add_fusion.meta, bf16[2,1088,512]{2,1,0:T(8,128)(2,1)} %get-tuple-element.62.mixed_ref, ...), custom_call_target="tpu_custom_call" | custom-call | flops 10066329600 | tf_op jit(solution)/shard_map/encoder_back/pallas_call | solution.py:318
  401.1 6.0 %copy.416 = bf16[2,1024,800]{1,2,0:T(8,128)(2,1)} copy(bf16[2,1024,800]{2,1,0:T(8,128)(2,1)} %get-tuple-element.52) | data formatting | bytes 6553600 | tf_op jit(solution)/shard_map/decoder_out/pallas_call | solution.py:318
  439.6 9.1 %collective-permute-done.49 = bf16[912,128]{1,0:T(8,128)(2,1)S(1)} collective-permute-done((bf16[912,128]{1,0:T(8,128)(2,1)S(1)}, bf16[912,128]{1,0:T(8,128)(2,1)S(1)}, u32[]{:S(2)}, u32[]{:S(2)}) %collective-permute-start.49) | collective-permute-done | bytes 233504 | tf_op jit(solution)/shard_map/ppermute | solution.py:373
  456.4 5.9 %copy.419.recv_ref = bf16[2,1024,800]{2,1,0:T(8,128)(2,1)} copy(bf16[2,1024,800]{1,2,0:T(8,128)(2,1)} %collective-permute-done.33) | data formatting | bytes 6553600 | tf_op jit(solution)/shard_map/ppermute | solution.py:373
  462.4 7.7 %fill_rows.3 = f32[4,1024,800]{2,1,0:T(8,128)} custom-call(s32[2]{0:T(128)} %pad_add_fusion.meta, bf16[2,1024,800]{2,1,0:T(8,128)(2,1)} %copy.419.recv_ref, f32[4,1024,800]{2,1,0:T(8,128)} %get-tuple-element.68.final_ref), custom_call_target="tpu_custom_call", output_to_operand_aliasing={{}: (2, {})} | custom-call | bytes 9830400 | tf_op jit(solution)/shard_map/fill_rows/pallas_call | solution.py:318
  470.1 14.6 %copy.422 = f32[1,4,1024,800]{2,3,1,0:T(8,128)} copy(f32[1,4,1024,800]{3,2,1,0:T(8,128)} %bitcast.191) | data formatting | bytes 26214400
  484.7 5.9 %copy.417.recv_ref = bf16[2,1024,800]{2,1,0:T(8,128)(2,1)} copy(bf16[2,1024,800]{1,2,0:T(8,128)(2,1)} %collective-permute-done.32) | data formatting | bytes 6553600 | tf_op jit(solution)/shard_map/ppermute | solution.py:373
  490.6 7.7 %fill_rows.2 = f32[4,1024,800]{2,1,0:T(8,128)} custom-call(s32[2]{0:T(128)} %pad_add_fusion.meta, bf16[2,1024,800]{2,1,0:T(8,128)(2,1)} %copy.417.recv_ref, f32[4,1024,800]{2,1,0:T(8,128)} %get-tuple-element.53.final_ref), custom_call_target="tpu_custom_call", output_to_operand_aliasing={{}: (2, {})} | custom-call | bytes 9830400 | tf_op jit(solution)/shard_map/fill_rows/pallas_call | solution.py:318
  498.3 14.6 %copy.421 = f32[1,4,1024,800]{2,3,1,0:T(8,128)} copy(f32[1,4,1024,800]{3,2,1,0:T(8,128)} %bitcast.190) | data formatting | bytes 26214400
  (313 shorter events, 211.5 us)
Async XLA Ops:
  2.0 108.1 %collective-permute-start.2 = (bf16[200,128]{1,0:T(8,128)(2,1)S(1)}, bf16[200,128]{1,0:T(8,128)(2,1)S(1)}, u32[]{:S(2)}, u32[]{:S(2)}) collective-permute-start(bf16[200,128]{1,0:T(8,128)(2,1)S(1)} %get-tuple-element.301), channel_id=1, source_target_pairs={{0,1},{1,0},{2,3},{3,2},{4,5},{5,4},{6,7},{7,6},{8,9},{9,8},{10,11... | collective-permute-start | bytes 153608 | tf_op jit(solution)/shard_map/ppermute | solution.py:373
  4.2 107.5 %collective-permute-start.3 = (bf16[200,128]{1,0:T(8,128)(2,1)S(1)}, bf16[200,128]{1,0:T(8,128)(2,1)S(1)}, u32[]{:S(2)}, u32[]{:S(2)}) collective-permute-start(bf16[200,128]{1,0:T(8,128)(2,1)S(1)} %get-tuple-element.301), channel_id=1, source_target_pairs={{0,2},{1,3},{2,0},{3,1},{4,6},{5,7},{6,4},{7,5},{8,10},{9,11},{10,... | collective-permute-start | bytes 153608 | tf_op jit(solution)/shard_map/ppermute | solution.py:373
  6.5 107.4 %collective-permute-start.4 = (bf16[200,128]{1,0:T(8,128)(2,1)S(1)}, bf16[200,128]{1,0:T(8,128)(2,1)S(1)}, u32[]{:S(2)}, u32[]{:S(2)}) collective-permute-start(bf16[200,128]{1,0:T(8,128)(2,1)S(1)} %get-tuple-element.301), channel_id=1, source_target_pairs={{0,3},{1,2},{2,1},{3,0},{4,7},{5,6},{6,5},{7,4},{8,11},{9,10},{10,... | collective-permute-start | bytes 153608 | tf_op jit(solution)/shard_map/ppermute | solution.py:373
  7.3 59.3 %collective-permute-start.14 = (s32[2,128]{1,0:T(2,128)S(1)}, s32[2,128]{1,0:T(2,128)S(1)}, u32[]{:S(2)}, u32[]{:S(2)}) collective-permute-start(s32[2,128]{1,0:T(2,128)S(1)} %get-tuple-element.322), channel_id=1, source_target_pairs={{0,4},{4,8},{8,12},{1,5},{5,9},{9,13},{2,6},{6,10},{10,14},{3,7},{... | collective-permute-start | bytes 3080 | tf_op jit(solution)/shard_map/ppermute | solution.py:462
  10.4 56.6 %collective-permute-start.15 = (s32[2,128]{1,0:T(2,128)S(1)}, s32[2,128]{1,0:T(2,128)S(1)}, u32[]{:S(2)}, u32[]{:S(2)}) collective-permute-start(s32[2,128]{1,0:T(2,128)S(1)} %get-tuple-element.323), channel_id=1, source_target_pairs={{4,0},{8,4},{12,8},{5,1},{9,5},{13,9},{6,2},{10,6},{14,10},{7,3},{... | collective-permute-start | bytes 3080 | tf_op jit(solution)/shard_map/ppermute | solution.py:463
  72.4 30.8 %collective-permute-start.9 = (f32[8,800]{1,0:T(8,128)S(1)}, f32[8,800]{1,0:T(8,128)S(1)}, u32[]{:S(2)}, u32[]{:S(2)}) collective-permute-start(f32[8,800]{1,0:T(8,128)S(1)} %select_maximum_fusion.1), channel_id=1, source_target_pairs={{0,16},{16,0},{1,17},{17,1},{2,18},{18,2},{3,19},{19,3},{4,20},{20... | collective-permute-start | bytes 76808 | tf_op jit(solution)/shard_map/ppermute | solution.py:373
  75.8 26.7 %collective-permute-start.13 = (f32[8,512]{1,0:T(8,128)S(1)}, f32[8,512]{1,0:T(8,128)S(1)}, u32[]{:S(2)}, u32[]{:S(2)}) collective-permute-start(f32[8,512]{1,0:T(8,128)S(1)} %bitcast.213), channel_id=1, source_target_pairs={{0,16},{16,0},{1,17},{17,1},{2,18},{18,2},{3,19},{19,3},{4,20},{20... | collective-permute-start | bytes 49160 | tf_op jit(solution)/shard_map/ppermute | solution.py:373
  109.5 23.7 %collective-permute-start.16 = (bf16[4,128,128]{2,1,0:T(8,128)(2,1)}, bf16[4,128,128]{2,1,0:T(8,128)(2,1)S(1)}, u32[]{:S(2)}, u32[]{:S(2)}) collective-permute-start(bf16[4,128,128]{2,1,0:T(8,128)(2,1)} %constant_dynamic-slice_fusion.8), channel_id=1, source_target_pairs={{0,1},{1,0},{2,3},{3,2},{4,5},{5,4},{6,7},{7,6},{8,9},{9,8},{10,11... | collective-permute-start | bytes 393224 | tf_op jit(solution)/shard_map/ppermute | solution.py:373
  110.1 24.5 %collective-permute-start.17 = (bf16[4,128,128]{2,1,0:T(8,128)(2,1)}, bf16[4,128,128]{2,1,0:T(8,128)(2,1)S(1)}, u32[]{:S(2)}, u32[]{:S(2)}) collective-permute-start(bf16[4,128,128]{2,1,0:T(8,128)(2,1)} %constant_dynamic-slice_fusion.8), channel_id=1, source_target_pairs={{0,2},{1,3},{2,0},{3,1},{4,6},{5,7},{6,4},{7,5},{8,10},{9,11},{10,... | collective-permute-start | bytes 393224 | tf_op jit(solution)/shard_map/ppermute | solution.py:373
  111.7 28.5 %collective-permute-start.18 = (bf16[4,128,128]{2,1,0:T(8,128)(2,1)}, bf16[4,128,128]{2,1,0:T(8,128)(2,1)S(1)}, u32[]{:S(2)}, u32[]{:S(2)}) collective-permute-start(bf16[4,128,128]{2,1,0:T(8,128)(2,1)} %constant_dynamic-slice_fusion.8), channel_id=1, source_target_pairs={{0,3},{1,2},{2,1},{3,0},{4,7},{5,6},{6,5},{7,4},{8,11},{9,10},{10,... | collective-permute-start | bytes 393224 | tf_op jit(solution)/shard_map/ppermute | solution.py:373
  113.9 107.6 %collective-permute-start = (bf16[2,80,800]{2,1,0:T(8,128)(2,1)}, bf16[2,80,800]{2,1,0:T(8,128)(2,1)}, u32[]{:S(2)}, u32[]{:S(2)}) collective-permute-start(bf16[2,80,800]{2,1,0:T(8,128)(2,1)} %get-tuple-element.289), channel_id=1, source_target_pairs={{0,4},{4,8},{8,12},{1,5},{5,9},{9,13},{2,6},{6,10},{10,14},{3,7},{... | collective-permute-start | bytes 768008 | tf_op jit(solution)/shard_map/ppermute | solution.py:462
  128.3 101.6 %collective-permute-start.1 = (bf16[2,80,800]{2,1,0:T(8,128)(2,1)}, bf16[2,80,800]{2,1,0:T(8,128)(2,1)}, u32[]{:S(2)}, u32[]{:S(2)}) collective-permute-start(bf16[2,80,800]{2,1,0:T(8,128)(2,1)} %get-tuple-element.288), channel_id=1, source_target_pairs={{4,0},{8,4},{12,8},{5,1},{9,5},{13,9},{6,2},{10,6},{14,10},{7,3},{... | collective-permute-start | bytes 768008 | tf_op jit(solution)/shard_map/ppermute | solution.py:463
  133.1 33.8 %collective-permute-start.31 = (bf16[2,48,800]{2,1,0:T(8,128)(2,1)}, bf16[2,48,800]{2,1,0:T(8,128)(2,1)}, u32[]{:S(2)}, u32[]{:S(2)}) collective-permute-start(bf16[2,48,800]{2,1,0:T(8,128)(2,1)} %get-tuple-element.287), channel_id=1, source_target_pairs={{4,0},{8,4},{12,8},{5,1},{9,5},{13,9},{6,2},{10,6},{14,10},{7,3},{... | collective-permute-start | bytes 460808 | tf_op jit(solution)/shard_map/ppermute | solution.py:463
  134.6 34.2 %collective-permute-start.30 = (bf16[2,48,800]{2,1,0:T(8,128)(2,1)S(1)}, bf16[2,48,800]{2,1,0:T(8,128)(2,1)}, u32[]{:S(2)}, u32[]{:S(2)}) collective-permute-start(bf16[2,48,800]{2,1,0:T(8,128)(2,1)S(1)} %get-tuple-element.286), channel_id=1, source_target_pairs={{0,4},{4,8},{8,12},{1,5},{5,9},{9,13},{2,6},{6,10},{10,14},{3,7},{... | collective-permute-start | bytes 460808 | tf_op jit(solution)/shard_map/ppermute | solution.py:462
  140.2 37.0 %collective-permute-start.5 = (bf16[4,200,128]{2,0,1:T(4,128)(2,1)}, bf16[4,200,128]{2,0,1:T(4,128)(2,1)}, u32[]{:S(2)}, u32[]{:S(2)}) collective-permute-start(bf16[4,200,128]{2,0,1:T(4,128)(2,1)} %copy-done.9), channel_id=1, source_target_pairs={{0,4},{4,0},{8,12},{12,8},{1,5},{5,1},{9,13},{13,9},{2,6},{6,2},{1... | collective-permute-start | bytes 614408 | tf_op jit(solution)/shard_map/ppermute | solution.py:373
  190.7 26.2 %collective-permute-start.27 = (bf16[4,32,800]{2,1,0:T(8,128)(2,1)}, bf16[4,32,800]{2,1,0:T(8,128)(2,1)S(1)}, u32[]{:S(2)}, u32[]{:S(2)}) collective-permute-start(bf16[4,32,800]{2,1,0:T(8,128)(2,1)} %bitcast_dynamic-update-slice_fusion.16), channel_id=1, source_target_pairs={{0,8},{4,12},{8,0},{12,4},{1,9},{5,13},{9,1},{13,5},{2,10},{6,14},... | collective-permute-start | bytes 614408 | tf_op jit(solution)/shard_map/ppermute | solution.py:373
  195.1 21.9 %collective-permute-start.28 = (bf16[4,32,800]{2,1,0:T(8,128)(2,1)}, bf16[4,32,800]{2,1,0:T(8,128)(2,1)}, u32[]{:S(2)}, u32[]{:S(2)}) collective-permute-start(bf16[4,32,800]{2,1,0:T(8,128)(2,1)} %bitcast_dynamic-update-slice_fusion.16), channel_id=1, source_target_pairs={{0,12},{4,8},{8,4},{12,0},{1,13},{5,9},{9,5},{13,1},{2,14},{6,10},... | collective-permute-start | bytes 614408 | tf_op jit(solution)/shard_map/ppermute | solution.py:373
  202.9 30.1 %collective-permute-start.8 = (bf16[800,512]{1,0:T(8,128)(2,1)}, bf16[800,512]{1,0:T(8,128)(2,1)}, u32[]{:S(2)}, u32[]{:S(2)}) collective-permute-start(bf16[800,512]{1,0:T(8,128)(2,1)} %bitcast.188), channel_id=1, source_target_pairs={{0,16},{16,0},{1,17},{17,1},{2,18},{18,2},{3,19},{19,3},{4,20},{20... | collective-permute-start | bytes 2457608 | tf_op jit(solution)/shard_map/ppermute | solution.py:373
  216.9 34.6 %collective-permute-start.22 = (bf16[4,512,512]{2,1,0:T(8,128)(2,1)}, bf16[4,512,512]{2,1,0:T(8,128)(2,1)}, u32[]{:S(2)}, u32[]{:S(2)}) collective-permute-start(bf16[4,512,512]{2,1,0:T(8,128)(2,1)} %reshape.112), channel_id=1, source_target_pairs={{0,16},{16,0},{1,17},{17,1},{2,18},{18,2},{3,19},{19,3},{4,20},{20... | collective-permute-start | bytes 6291464 | tf_op jit(solution)/shard_map/ppermute | solution.py:373
  381.9 29.5 %collective-permute-start.42 = (bf16[128,800]{1,0:T(8,128)(2,1)}, bf16[128,800]{1,0:T(8,128)(2,1)}, u32[]{:S(2)}, u32[]{:S(2)}) collective-permute-start(bf16[128,800]{1,0:T(8,128)(2,1)} %select_convert_fusion.2), channel_id=1, source_target_pairs={{0,16},{16,0},{1,17},{17,1},{2,18},{18,2},{3,19},{19,3},{4,20},{20... | collective-permute-start | bytes 614408 | tf_op jit(solution)/shard_map/ppermute | solution.py:373
  389.3 26.5 %collective-permute-start.43 = (bf16[128,800]{1,0:T(8,128)(2,1)}, bf16[128,800]{1,0:T(8,128)(2,1)}, u32[]{:S(2)}, u32[]{:S(2)}) collective-permute-start(bf16[128,800]{1,0:T(8,128)(2,1)} %select_convert_fusion.1), channel_id=1, source_target_pairs={{0,16},{16,0},{1,17},{17,1},{2,18},{18,2},{3,19},{19,3},{4,20},{20... | collective-permute-start | bytes 614408 | tf_op jit(solution)/shard_map/ppermute | solution.py:373
  393.1 25.8 %collective-permute-start.44 = (bf16[4,128,512]{2,1,0:T(8,128)(2,1)}, bf16[4,128,512]{2,1,0:T(8,128)(2,1)}, u32[]{:S(2)}, u32[]{:S(2)}) collective-permute-start(bf16[4,128,512]{2,1,0:T(8,128)(2,1)} %select_convert_fusion), channel_id=1, source_target_pairs={{0,16},{16,0},{1,17},{17,1},{2,18},{18,2},{3,19},{19,3},{4,20},{20... | collective-permute-start | bytes 1572872 | tf_op jit(solution)/shard_map/ppermute | solution.py:373
  401.1 55.3 %collective-permute-start.33 = (bf16[2,1024,800]{1,2,0:T(8,128)(2,1)}, bf16[2,1024,800]{1,2,0:T(8,128)(2,1)}, u32[]{:S(2)}, u32[]{:S(2)}) collective-permute-start(bf16[2,1024,800]{1,2,0:T(8,128)(2,1)} %copy.418), channel_id=1, source_target_pairs={{0,16},{16,0},{1,17},{17,1},{2,18},{18,2},{3,19},{19,3},{4,20},{20... | collective-permute-start | bytes 9830408 | tf_op jit(solution)/shard_map/ppermute | solution.py:373
  409.7 75.0 %collective-permute-start.32 = (bf16[2,1024,800]{1,2,0:T(8,128)(2,1)}, bf16[2,1024,800]{1,2,0:T(8,128)(2,1)}, u32[]{:S(2)}, u32[]{:S(2)}) collective-permute-start(bf16[2,1024,800]{1,2,0:T(8,128)(2,1)} %copy.416), channel_id=1, source_target_pairs={{0,16},{16,0},{1,17},{17,1},{2,18},{18,2},{3,19},{19,3},{4,20},{20... | collective-permute-start | bytes 9830408 | tf_op jit(solution)/shard_map/ppermute | solution.py:373
  (55 other events, 623.8 us)

commit v2 on v1

v2 whole, which is shorter than its diff:
```python
import functools
import math

import jax
import jax.numpy as jnp
from jax import lax
from jax.experimental import pallas as pl
from jax.experimental.pallas import tpu as pltpu
from jax.sharding import PartitionSpec as P

SPACING = 16
EPSILON = 1e-05
BF = jnp.bfloat16
F32 = jnp.float32
LANES = 512
TILE = 128
CHUNK = 256
BLOCK = 16
PIECE = 208
ROOT = math.sqrt(2.0 / math.pi)
CUBIC = 0.044715
E_OFFSETS = tuple(SPACING * (k - 2) for k in range(5))
D_OFFSETS = (-2, -1, 0)
VMEM = 60 * 1024 * 1024
FREE = 120
COT_TURNS = (96, 48)


def dot(a, b):
    return lax.dot_general(a, b, (((1,), (0,)), ((), ())), preferred_element_type=F32)


def dot_nt(a, b):
    return lax.dot_general(a, b, (((1,), (1,)), ((), ())), preferred_element_type=F32)


def pair(column):
    return jnp.concatenate([column, column], axis=1)


def row_sum(values):
    return jnp.sum(values, axis=0, keepdims=True)


def moments(get, count):
    total = square = None
    for j in range(0, count, BLOCK):
        x = get(j)
        total = x if total is None else total + x
        square = x * x if square is None else square + x * x
    center = row_sum(total) * (1.0 / count)
    inverse = lax.rsqrt(row_sum(square) * (1.0 / count) - center * center + EPSILON)
    return center * inverse, inverse


def gate(half):
    square = half * half
    return jnp.tanh(half * (2 * ROOT + (8 * CUBIC * ROOT) * square)), square


def slope(half, tanh, square):
    return (1.0 + tanh) * (0.5 + (half - half * tanh) * (ROOT + (12 * CUBIC * ROOT) * square))


def spread(target, source, columns, *whole):
    for n, c in enumerate(columns):
        value = jnp.broadcast_to(source[:, c : c + 1], target.shape[1:])
        target[n] = value if n in [w - 1 for w in whole] else 0.5 * value


def param(ref, n, j):
    return pair(ref[n, j : j + BLOCK, :])


def placed(sel, a_ref, b_ref, lo):
    parts = []
    for q in range(a_ref.shape[0]):
        part = jnp.where(sel, a_ref[q, lo : lo + PIECE, :], b_ref[q, lo : lo + PIECE, :])
        parts.append(part.astype(F32)[:200])
    return jnp.concatenate(parts, axis=0).astype(BF)


def tap_of(sel, a_ref, b_ref, tap, inner):
    q = tap % 4
    first, second = a_ref[q, :inner, :], b_ref[q, :inner, :]
    return jnp.where(sel, first, second) if tap < 4 else jnp.where(sel, second, first)


def drive(streams):
    streams = list(streams)
    while streams:
        for stream in tuple(streams):
            try:
                next(stream)
            except StopIteration:
                streams.remove(stream)


def tiles_of(step):
    return jnp.where(step == 0, 1, 2 * step), jnp.where(step == 0, 10, 2 * step + 1)


def at_tile(a, count=1):
    return pl.ds(pl.multiple_of(a * TILE, TILE), count * TILE)


def code_rows(code_ref, n, a, offsets):
    window = code_ref[n, :, at_tile(a - 1, 3)]
    here = window[:, TILE : 2 * TILE]
    return [(window[:, TILE + o : 2 * TILE + o] == here).astype(F32) for o in offsets], (here > 0.5).astype(F32)


def taps(cat_ref, ref, code_ref, n, step, offsets, count):
    kept = []
    for half, a in enumerate(tiles_of(step)):
        masks, keep = code_rows(code_ref, n, a, offsets)
        kept.append(keep)
        lanes = slice(n * CHUNK + half * TILE, n * CHUNK + (half + 1) * TILE)
        window = ref[n, :, at_tile(a - 1, 3)]
        for k, offset in enumerate(offsets):
            piece = window[:, TILE + offset : 2 * TILE + offset]
            if offset:
                piece = piece * masks[k].astype(BF)
            cat_ref[k * count : (k + 1) * count, lanes] = piece
    return jnp.concatenate(kept, axis=1)


def row_taps(cat_ref, ref, col_ref, n, step, offsets):
    for half, a in enumerate(tiles_of(step)):
        here = col_ref[n, at_tile(a), :]
        rows = slice(n * CHUNK + half * TILE, n * CHUNK + (half + 1) * TILE)
        for k, offset in enumerate(offsets):
            there = pl.ds(pl.multiple_of(a * TILE + offset, BLOCK), TILE)
            piece = ref[n, there, :]
            if offset:
                mask = (col_ref[n, there, :] == here).astype(BF)
                piece = piece * jnp.concatenate([mask] * (LANES // TILE), axis=1)
            cat_ref[rows, k * LANES : (k + 1) * LANES] = piece


def put_rows(ext_ref, n, step, values):
    turned = jnp.transpose(values[...])
    for half, a in enumerate(tiles_of(step)):
        ext_ref[n, at_tile(a), 0 : turned.shape[1]] = turned[half * TILE : (half + 1) * TILE, :]


def keep_row(code_ref, n, step):
    return jnp.concatenate([(code_ref[n, :, at_tile(a)] > 0.5).astype(F32) for a in tiles_of(step)], axis=1)


def put(ext_ref, n, step, values):
    for half, a in enumerate(tiles_of(step)):
        ext_ref[n, :, at_tile(a)] = values[:, half * TILE : (half + 1) * TILE]


def blank_ends(ext_ref):
    for a in (0, 11):
        ext_ref[:, :, a * TILE : (a + 1) * TILE] = jnp.zeros(ext_ref.shape[:2] + (TILE,), BF)


def from_sums(total, square, count):
    center = row_sum(total) * (1.0 / count)
    inverse = lax.rsqrt(row_sum(square) * (1.0 / count) - center * center + EPSILON)
    return center * inverse, inverse


def biased(hid_ref, product, ph, n):
    count = hid_ref.shape[0]
    total = square = None
    for j in range(0, count, BLOCK):
        x = product[j : j + BLOCK, :] + param(ph, n, j)
        hid_ref[j : j + BLOCK, :] = x
        total = x if total is None else total + x
        square = x * x if square is None else square + x * x
    return from_sums(total, square, count)


def activate(hid_ref, stats, ph, gain, bias, out_ref, xh_ref, dg_ref, inv_ref):
    shift, inverse = stats
    inv_ref[...] = jnp.broadcast_to(inverse, inv_ref.shape)
    for j in range(0, hid_ref.shape[0], BLOCK):
        scaled = hid_ref[j : j + BLOCK, :] * inverse - shift
        half = scaled * param(ph, gain, j) + param(ph, bias, j)
        tanh, square = gate(half)
        out_ref[j : j + BLOCK, :] = (half + half * tanh).astype(BF)
        xh_ref[j : j + BLOCK, :] = scaled.astype(BF)
        dg_ref[j : j + BLOCK, :] = slope(half, tanh, square).astype(BF)


def first_of(x_ref, stats, pd, gain, out_ref, slope_ref=None):
    shift, inverse = stats
    for j in range(0, x_ref.shape[0], BLOCK):
        scaled = x_ref[j : j + BLOCK, :] * inverse - shift
        half = scaled * param(pd, gain, j) + param(pd, gain + 1, j)
        tanh, square = gate(half)
        out_ref[j : j + BLOCK, :] = (half + half * tanh).astype(BF)
        if slope_ref is not None:
            slope_ref[j : j + BLOCK, :] = slope(half, tanh, square)


def moments_of(x_ref):
    return moments(lambda j: x_ref[j : j + BLOCK, :], x_ref.shape[0])


def halves(values):
    return values[:, :TILE] + values[:, TILE:]


def norm_back(grad, xh_ref, dg_ref, inverse, ph, gain, low_ref, wide_ref, acc, base):
    count = low_ref.shape[0]
    first = second = None
    for j in range(0, count, BLOCK):
        down = grad[j : j + BLOCK, :] * dg_ref[j : j + BLOCK, :].astype(F32)
        cross = down * xh_ref[j : j + BLOCK, :].astype(F32)
        acc[base, j : j + BLOCK, :] += halves(cross)
        acc[base + 1, j : j + BLOCK, :] += halves(down)
        g = param(ph, gain, j)
        weighted = down * g
        wide_ref[j : j + BLOCK, :] = weighted
        first = weighted if first is None else first + weighted
        second = cross * g if second is None else second + cross * g
    twice = inverse * 2.0
    first = row_sum(first) * (twice * (1.0 / count))
    second = row_sum(second) * (twice * (1.0 / count))
    for j in range(0, count, BLOCK):
        result = wide_ref[j : j + BLOCK, :] * twice - first - xh_ref[j : j + BLOCK, :].astype(F32) * second
        low_ref[j : j + BLOCK, :] = result.astype(BF)
        acc[base + 2, j : j + BLOCK, :] += halves(result)


def own_rows(pick_ref, values):
    return dot(pick_ref[...], values).astype(BF)


def columns(target, lane, acc, order):
    count = acc.shape[1]
    for n, k in enumerate(order):
        target[0:count, lane + n : lane + n + 1] = jnp.sum(acc[k], axis=1, keepdims=True)


def clear(step, *refs):
    @pl.when(step <= 1)
    def _():
        for ref in refs:
            ref[...] = jnp.zeros_like(ref)


def turned(tile, by):
    return pltpu.roll(tile, by, 1) if by else tile


def fetch(step, target, own_ref, before_ref, after_ref, turns):
    @pl.when(step == 0)
    def _():
        width = target.shape[1]
        for n in range(2):
            target[n, :, 0:TILE] = turned(before_ref[n, 0:width, :].astype(F32), turns[0])
            target[n, :, TILE:] = turned(after_ref[n, 0:width, :].astype(F32), turns[1])

    @pl.when(step > 0)
    def _():
        target[...] = own_ref[...]


def encoder_in(meta, tok_ref, before_ref, after_ref, a_ref, b_ref, eye_ref, pd_ref, ph_ref,
               sec_ref, xh_ref, dg_ref, inv_ref, wi, pd, ph, x_s, first_s, hid_s, sec_s):
    step = pl.program_id(0)

    @pl.when(step == 0)
    def _():
        spread(pd, pd_ref, (0, 1))
        spread(ph, ph_ref, (0, 1, 2), 1)
        wi[...] = dot_nt(eye_ref[...], placed(meta[0] == 0, a_ref, b_ref, 0)).astype(BF)
        sec_ref[...] = jnp.zeros_like(sec_ref)

    fetch(step, x_s, tok_ref, before_ref, after_ref, (0, 0))

    def stream(n):
        first_of(x_s.at[n], moments_of(x_s.at[n]), pd, 0, first_s.at[n])
        product = dot(wi[...], first_s[n])
        yield
        stats = biased(hid_s.at[n], product, ph, 0)
        activate(hid_s.at[n], stats, ph, 1, 2, sec_s.at[n], xh_ref.at[n], dg_ref.at[n], inv_ref.at[n])
        put_rows(sec_ref, n, step, sec_s.at[n])

    drive(stream(n) for n in range(2))


def encoder_out(meta, sec_ref, code_ref, col_ref, tok_ref, before_ref, after_ref, a_ref, b_ref, ao_ref, bo_ref, ai_ref, bi_ref,
                eye_ref, pick_ref, pd_ref, ph_ref,
                out_ref, xh3_ref, dg3_ref, inv3_ref, third_ref, secd_ref, xh2_ref, dg2_ref, inv2_ref,
                wc, wo, wi, pd, ph, cat, hid_s, third_s, first_s, sec_s):
    step = pl.program_id(0)
    width = tok_ref.shape[1]
    inner = eye_ref.shape[0]

    @pl.when(step == 0)
    def _():
        spread(pd, pd_ref, (2, 3, 4), 1)
        spread(ph, ph_ref, (3, 4, 5, 6, 7, 8), 1, 4)
        sel = meta[0] == 0
        wc[...] = jnp.zeros_like(wc)
        for k in range(5):
            wc[:, k * LANES : k * LANES + inner] = dot_nt(eye_ref[...], tap_of(sel, a_ref, b_ref, k, inner)).astype(BF)
        wo[...] = dot_nt(placed(sel, ao_ref, bo_ref, 0), eye_ref[...]).astype(BF)
        wi[...] = dot_nt(eye_ref[...], placed(sel, bi_ref, ai_ref, 0)).astype(BF)
        blank_ends(secd_ref)

    fetch(step, out_ref, tok_ref, before_ref, after_ref, (0, 0))

    def stream(n):
        row_taps(cat, sec_ref, col_ref, n, step, E_OFFSETS)
        keep = keep_row(code_ref, n, step)
        product = dot_nt(wc[...], cat[n * CHUNK : (n + 1) * CHUNK, :])
        yield
        stats = biased(hid_s.at[n], product, ph, 0)
        activate(hid_s.at[n], stats, ph, 1, 2, third_s.at[n], xh3_ref.at[n], dg3_ref.at[n], inv3_ref.at[n])
        product = dot(wo[...], third_s[n])
        third_ref[n] = own_rows(pick_ref, third_s[n])
        yield
        kept = jnp.broadcast_to(keep, (BLOCK, CHUNK))
        total = square = None
        for j in range(0, width, BLOCK):
            x = out_ref[n, j : j + BLOCK, :] + kept * (product[j : j + BLOCK, :] + param(pd, 0, j))
            out_ref[n, j : j + BLOCK, :] = x
            total = x if total is None else total + x
            square = x * x if square is None else square + x * x
        first_of(out_ref.at[n], from_sums(total, square, width), pd, 1, first_s.at[n])
        product = dot(wi[...], first_s[n])
        yield
        stats = biased(hid_s.at[n], product, ph, 3)
        activate(hid_s.at[n], stats, ph, 4, 5, sec_s.at[n], xh2_ref.at[n], dg2_ref.at[n], inv2_ref.at[n])
        put(secd_ref, n, step, sec_s.at[n])

    drive(stream(n) for n in range(2))


def decoder_out(meta, sec_ref, code_ref, in_ref, cot_ref, before_ref, after_ref, a_ref, b_ref, ao_ref, bo_ref, eye_ref, pick_ref,
                pd_ref, ph_ref,
                mine_ref, other_ref, mixed_ref, go_ref, gc_ref,
                wc, wo, wob, pd, ph, cat, hid_s, third_s, cot_f, cot_s, low_s, xh_s, dg_s, inv_s, accd, acch):
    step = pl.program_id(0)
    width = in_ref.shape[1]
    inner = eye_ref.shape[0]

    @pl.when(step == 0)
    def _():
        spread(pd, pd_ref, (5,), 1)
        spread(ph, ph_ref, (9, 10, 11), 1)
        sel = meta[0] == 0
        for k in range(3):
            wc[:, k * inner : (k + 1) * inner] = dot_nt(eye_ref[...], tap_of(sel, a_ref, b_ref, 5 + k, inner)).astype(BF)
        outer = placed(sel, bo_ref, ao_ref, 0)
        wo[...] = dot_nt(outer, eye_ref[...]).astype(BF)
        wob[...] = dot_nt(eye_ref[...], outer).astype(BF)
        blank_ends(mixed_ref)

    clear(step, go_ref, gc_ref, accd, acch)
    fetch(step, cot_f, cot_ref, before_ref, after_ref, COT_TURNS)
    encoder_side = meta[0] == 0

    def stream(n):
        lanes = slice(n * CHUNK, (n + 1) * CHUNK)
        kept = jnp.broadcast_to(keep_row(code_ref, n, step), (BLOCK, CHUNK))
        for j in range(0, width, BLOCK):
            branch = kept * cot_f[n, j : j + BLOCK, :]
            accd[0, j : j + BLOCK, :] += halves(branch)
            cot_s[j : j + BLOCK, lanes] = branch.astype(BF)
        taps(cat, sec_ref, code_ref, n, step, D_OFFSETS, inner)
        product = dot(wc[...], cat[:, lanes])
        grad = dot(wob[...], cot_s[:, lanes])
        yield
        stats = biased(hid_s.at[n], product, ph, 0)
        activate(hid_s.at[n], stats, ph, 1, 2, third_s.at[n], xh_s.at[n], dg_s.at[n], inv_s.at[n])
        product = dot(wo[...], third_s[n])
        norm_back(grad, xh_s.at[n], dg_s.at[n], stats[1], ph, 1, low_s.at[n], hid_s.at[n], acch, 0)
        put(mixed_ref, n, step, low_s.at[n])
        yield
        for j in range(0, width, BLOCK):
            x = in_ref[n, j : j + BLOCK, :]
            y = x + kept * (product[j : j + BLOCK, :] + param(pd, 0, j))
            mine_ref[n, j : j + BLOCK, :] = jnp.where(encoder_side, x, y)
            other_ref[n, j : j + BLOCK, :] = jnp.where(encoder_side, y, x).astype(BF)

    drive(stream(n) for n in range(2))
    picked = own_rows(pick_ref, jnp.concatenate([third_s[0], third_s[1], low_s[0], low_s[1]], axis=1))
    go_ref[...] += dot_nt(cot_s[...], picked[:, : 2 * CHUNK])
    gc_ref[...] += dot_nt(cat[...], picked[:, 2 * CHUNK :])

    @pl.when(step == 4)
    def _():
        columns(go_ref, FREE, accd, (0,))
        columns(go_ref, FREE + 1, acch, (0, 1, 2))


def inner_back(n, grad_second, xh2_ref, dg2_ref, inv2_ref, in_ref, wib, pd, ph, hid_s, low_s, first_s, dg1_s, acch, accd, finish):
    lanes = slice(n * CHUNK, (n + 1) * CHUNK)
    width = in_ref.shape[1]
    stats = shift, inverse = moments_of(in_ref.at[n])
    first_of(in_ref.at[n], stats, pd, 0, first_s.at[:, lanes], dg1_s.at[n])
    norm_back(grad_second, xh2_ref.at[n], dg2_ref.at[n], inv2_ref[n, 0:1, :], ph, 0, low_s.at[n], hid_s.at[n], acch, 0)
    grad = dot(wib[...], low_s[n])
    yield
    first = second = None
    for j in range(0, width, BLOCK):
        scaled = in_ref[n, j : j + BLOCK, :] * inverse - shift
        down = grad[j : j + BLOCK, :] * dg1_s[n, j : j + BLOCK, :]
        cross = down * scaled
        accd[0, j : j + BLOCK, :] += halves(cross)
        accd[1, j : j + BLOCK, :] += halves(down)
        g = param(pd, 0, j)
        weighted = down * g
        dg1_s[n, j : j + BLOCK, :] = weighted
        first = weighted if first is None else first + weighted
        second = cross * g if second is None else second + cross * g
    twice = inverse * 2.0
    first = row_sum(first) * (twice * (1.0 / width))
    second = row_sum(second) * (twice * (1.0 / width))
    for j in range(0, width, BLOCK):
        scaled = in_ref[n, j : j + BLOCK, :] * inverse - shift
        finish(j, dg1_s[n, j : j + BLOCK, :] * twice - first - scaled * second)


def decoder_back(meta, mixed_ref, code_ref, xh2_ref, dg2_ref, inv2_ref, in_ref, cot_ref, before_ref, after_ref,
                 xh3_ref, dg3_ref, inv3_ref, third_ref, a_ref, b_ref, ai_ref, bi_ref, ao_ref, bo_ref, eye_ref, pick_ref,
                 pd_ref, ph_ref,
                 grad_ref, low3_ref, gi_ref, go_ref,
                 wc, wib, wob, pd, ph, cat, hid_s, low_s, low3_s, first_s, branch_s, dg1_s, accd, acch):
    step = pl.program_id(0)
    inner = eye_ref.shape[0]

    @pl.when(step == 0)
    def _():
        spread(pd, pd_ref, (3, 4))
        spread(ph, ph_ref, (7, 4))
        sel = meta[0] == 0
        for k in range(3):
            wc[:, k * inner : (k + 1) * inner] = dot_nt(tap_of(sel, a_ref, b_ref, 5 + k, inner), eye_ref[...]).astype(BF)
        wib[...] = dot_nt(placed(sel, bi_ref, ai_ref, 0), eye_ref[...]).astype(BF)
        wob[...] = dot_nt(eye_ref[...], placed(sel, ao_ref, bo_ref, 0)).astype(BF)
        low3_ref[...] = jnp.zeros_like(low3_ref)

    clear(step, gi_ref, go_ref, accd, acch)
    fetch(step, grad_ref, cot_ref, before_ref, after_ref, COT_TURNS)

    def stream(n):
        lanes = slice(n * CHUNK, (n + 1) * CHUNK)
        keep = taps(cat, mixed_ref, code_ref, n, step, tuple(-o for o in D_OFFSETS), inner)
        kept = jnp.broadcast_to(keep, (BLOCK, CHUNK))
        grad = dot(wc[...], cat[:, lanes])
        yield

        def finish(j, value):
            value = grad_ref[n, j : j + BLOCK, :] + value
            grad_ref[n, j : j + BLOCK, :] = value
            branch = kept * value
            accd[2, j : j + BLOCK, :] += halves(branch)
            branch_s[j : j + BLOCK, lanes] = branch.astype(BF)

        yield from inner_back(
            n, grad, xh2_ref, dg2_ref, inv2_ref, in_ref, wib, pd, ph, hid_s, low_s, first_s, dg1_s, acch, accd, finish
        )
        grad = dot(wob[...], branch_s[:, lanes])
        yield
        norm_back(grad, xh3_ref.at[n], dg3_ref.at[n], inv3_ref[n, 0:1, :], ph, 1, low3_s.at[n], hid_s.at[n], acch, 3)
        put_rows(low3_ref, n, step, low3_s.at[n])

    drive(stream(n) for n in range(2))
    low = own_rows(pick_ref, jnp.concatenate([low_s[0], low_s[1]], axis=1))
    third = jnp.concatenate([third_ref[n] for n in range(2)], axis=1)
    gi_ref[...] += dot_nt(first_s[...], low)
    go_ref[...] += dot_nt(branch_s[...], third)

    @pl.when(step == 4)
    def _():
        columns(gi_ref, FREE, accd, (0, 1))
        columns(gi_ref, FREE + 2, acch, (0, 1, 2))
        columns(go_ref, FREE, accd, (2,))
        columns(go_ref, FREE + 1, acch, (3, 4, 5))


def encoder_back(meta, mixed_ref, sec_ref, col_ref, xh2_ref, dg2_ref, inv2_ref, in_ref, later_ref, a_ref, b_ref,
                 ai_ref, bi_ref, eye_ref, pick_ref, pd_ref, ph_ref,
                 mine_ref, other_ref, gi_ref, gc_ref,
                 wc, wib, pd, ph, cat, catw, gc_s, hid_s, low_s, first_s, dg1_s, accd, acch):
    step = pl.program_id(0) + 1
    inner = eye_ref.shape[0]

    @pl.when(step == 1)
    def _():
        spread(pd, pd_ref, (0, 1))
        spread(ph, ph_ref, (1,))
        sel = meta[0] == 0
        wc[...] = jnp.zeros_like(wc)
        for k in range(5):
            wc[:, k * LANES : k * LANES + inner] = dot_nt(tap_of(sel, a_ref, b_ref, k, inner), eye_ref[...]).astype(BF)
        wib[...] = dot_nt(placed(sel, ai_ref, bi_ref, 0), eye_ref[...]).astype(BF)

    clear(step, gi_ref, gc_s, accd, acch)
    encoder_side = meta[0] == 0

    def stream(n):
        lanes = slice(n * CHUNK, (n + 1) * CHUNK)
        row_taps(cat, mixed_ref, col_ref, n, step, tuple(-o for o in E_OFFSETS))
        grad = dot_nt(wc[...], cat[lanes, :])
        yield

        def finish(j, value):
            later = later_ref[n, j : j + BLOCK, :]
            value = later + value
            mine_ref[n, j : j + BLOCK, :] = jnp.where(encoder_side, value, later)
            other_ref[n, j : j + BLOCK, :] = jnp.where(encoder_side, later, value).astype(BF)

        yield from inner_back(
            n, grad, xh2_ref, dg2_ref, inv2_ref, in_ref, wib, pd, ph, hid_s, low_s, first_s, dg1_s, acch, accd, finish
        )
        row_taps(catw, sec_ref, col_ref, n, step, E_OFFSETS)

    drive(stream(n) for n in range(2))
    low = own_rows(pick_ref, jnp.concatenate([low_s[0], low_s[1]], axis=1))
    mixed = jnp.concatenate(
        [dot_nt(pick_ref[...], mixed_ref[n, at_tile(2 * step, 2), 0:inner]).astype(BF) for n in range(2)], axis=1
    )
    gi_ref[...] += dot_nt(first_s[...], low)
    gc_s[...] += dot(mixed, catw[...])

    @pl.when(step == 4)
    def _():
        columns(gi_ref, FREE, accd, (0, 1))
        columns(gi_ref, FREE + 2, acch, (0, 1, 2))
        for k in range(5):
            gc_ref[k * inner : (k + 1) * inner, :] = jnp.transpose(gc_s[:, k * LANES : k * LANES + inner])


def fill_rows(meta, recv_ref, final_ref, out_ref):
    del meta, final_ref
    out_ref[...] = recv_ref[...].astype(F32)


def pack_edges(meta, tok_last, cot_last, tok_first, cot_first, code_last, code_first, tail_ref, head_ref):
    del meta
    width = tok_last.shape[1]
    lane = lax.broadcasted_iota(jnp.int32, (width, TILE), 1)
    for n in range(2):
        tail_ref[n, 0:width, :] = jnp.where(lane < 32, turned(cot_last[n], 32), tok_last[n]).astype(BF)
        head_ref[n, 0:width, :] = jnp.where(lane < 80, tok_first[n], turned(cot_first[n], 80)).astype(BF)
        tail_ref[n, width:, :] = jnp.broadcast_to(code_last[n], (BLOCK, TILE)).astype(BF)
        head_ref[n, width:, :] = jnp.broadcast_to(code_first[n], (BLOCK, TILE)).astype(BF)


def place_weights(place, own_ref, *refs):
    out_ref = refs[-1]
    for q in range(4):
        out_ref[q, :, at_tile(place[1])] = own_ref[q]
    for by in range(4):
        for slot in range(1, 4):
            out_ref[place[0] ^ by, :, at_tile(place[1] ^ slot)] = refs[by][slot - 1]


def pack_grads(meta, gie, goe, gce, gid, god, gcd, kept_ref, sent_ref):
    encoder_side = meta[0] == 0
    width, most = gie.shape[0], 4 * (gce.shape[0] // 5)
    pieces = [(gie[...], gid[...]), (goe[...], god[...])]
    pieces.append((gce[0:most, :], jnp.concatenate([gce[most:, :], gcd[...]], axis=0)))
    start = 0
    for e, d in pieces:
        rows = slice(start, start + e.shape[0])
        start += e.shape[0]
        kept_ref[rows, :] = jnp.where(encoder_side, e, d)
        sent_ref[rows, :] = jnp.where(encoder_side, d, e).astype(BF)


def call(body, meta, grid, ins, outs, scratch=(), aliases=None, name=None, us=3):
    return pl.pallas_call(
        body,
        grid_spec=pltpu.PrefetchScalarGridSpec(
            num_scalar_prefetch=1,
            grid=grid,
            in_specs=[s for _, s in ins],
            out_specs=[s for _, s in outs],
            scratch_shapes=list(scratch),
        ),
        out_shape=[s for s, _ in outs],
        input_output_aliases=aliases or {},
        compiler_params=pltpu.CompilerParams(
            dimension_semantics=("arbitrary",) * len(grid), vmem_limit_bytes=VMEM
        ),
        cost_estimate=pl.CostEstimate(flops=int(us * 1.0e9), bytes_accessed=int(us * 3.5e6), transcendentals=0),
        name=name,
    )(meta, *[a for a, _ in ins])


def per_step(array, steps=5):
    first = array.shape[0] // 2 - steps
    return (array, pl.BlockSpec((2,) + array.shape[1:], lambda c, m: (c + first, 0, 0)))


def own_index(c, m):
    return (m[0], 0, jnp.maximum(c - 1, 0))


def rows_chunk(array):
    return (array, pl.BlockSpec((2, array.shape[1], CHUNK), own_index))


def fixed(array):
    zeros = (0,) * array.ndim
    return (array, pl.BlockSpec(array.shape, lambda c, m: zeros))


def part(array, rows, index):
    return (array, pl.BlockSpec((array.shape[0], rows, array.shape[2]), lambda c, m: (0, index, 0)))


def out_chunks(rows, dtype):
    return (jax.ShapeDtypeStruct((10, rows, CHUNK), dtype), pl.BlockSpec((2, rows, CHUNK), lambda c, m: (c, 0, 0)))


def out_fixed(shape, dtype=F32):
    zeros = (0,) * len(shape)
    return (jax.ShapeDtypeStruct(shape, dtype), pl.BlockSpec(shape, lambda c, m: zeros))


def flip(x, axis, by):
    count = lax.axis_size(axis)
    return lax.ppermute(x, axis, [(i, i ^ by) for i in range(count)])


def gather(x, axis):
    me = lax.axis_index(axis)
    count = lax.axis_size(axis)
    result = jnp.zeros((count,) + x.shape, x.dtype)
    result = lax.dynamic_update_index_in_dim(result, x, me, 0)
    for by in range(1, count):
        result = lax.dynamic_update_index_in_dim(result, flip(x, axis, by), me ^ by, 0)
    return result


def gather_lanes(x, axis):
    me = lax.axis_index(axis)
    count = lax.axis_size(axis)
    lanes = x.shape[-1]
    result = jnp.zeros(x.shape[:-1] + (count * lanes,), x.dtype)
    result = lax.dynamic_update_slice_in_dim(result, x, me * lanes, 1)
    for by in range(1, count):
        result = lax.dynamic_update_slice_in_dim(result, flip(x, axis, by), (me ^ by) * lanes, 1)
    return result


def spread_over(x, axis, beside):
    count = lax.axis_size(axis)
    me = lax.axis_index(axis)
    parts = x.reshape((count, x.shape[0] // count) + x.shape[1:])
    low = parts.astype(BF)
    arrived = [
        flip(lax.dynamic_index_in_dim(low, me ^ by, 0, keepdims=False), axis, by) for by in range(1, count)
    ]
    arrived, beside = lax.optimization_barrier((arrived, beside))
    total = lax.dynamic_index_in_dim(parts, me, 0, keepdims=False)
    for part_of in arrived:
        total = total + part_of.astype(F32)
    return total.astype(BF), beside


def collect_over(x, axis, beside):
    me = lax.axis_index(axis)
    count = lax.axis_size(axis)
    arrived = [flip(x, axis, by) for by in range(1, count)]
    arrived, beside = lax.optimization_barrier((arrived, beside))
    result = jnp.zeros((count,) + x.shape, x.dtype)
    result = lax.dynamic_update_index_in_dim(result, x, me, 0)
    for by in range(1, count):
        result = lax.dynamic_update_index_in_dim(result, arrived[by - 1], me ^ by, 0)
    return result.reshape((count * x.shape[0],) + x.shape[1:]), beside


def pad_to(x, axis, size):
    widths = [(0, 0)] * x.ndim
    widths[axis] = (0, size - x.shape[axis])
    return jnp.pad(x, widths)


def on_device(
    tokens, segments, pad_mask, cotangent, gain_first, bias_first, weight_inner, bias_inner, gain_middle, bias_middle,
    weight_conv_encoder, weight_conv_decoder, bias_conv, gain_last, bias_last, weight_outer, bias_outer,
):
    pipe, seq, tensor = (lax.axis_index(a) for a in ("pipe", "seq", "tensor"))
    n_pipe, n_seq, n_tensor = (lax.axis_size(a) for a in ("pipe", "seq", "tensor"))
    rows_all, length, width = tokens.shape
    rows = rows_all // n_pipe
    loc = weight_conv_encoder.shape[2]
    inner = weight_conv_encoder.shape[1]
    lanes = LANES // n_tensor
    encoder_side = pipe == 0
    meta = jnp.stack([pipe, tensor * loc]).astype(jnp.int32)
    tokens_t, cotangent_t = jnp.transpose(tokens, (0, 2, 1)), jnp.transpose(cotangent, (0, 2, 1))

    def mine_rows(array):
        return lax.dynamic_slice_in_dim(array, pipe * rows, rows, 0)

    codes = (mine_rows(jnp.where(pad_mask == 1, segments + 1, 0)).astype(F32) + 1.0)[:, None, :]
    last = length // TILE - 1

    def edge_tile(array, row, index):
        return (array, pl.BlockSpec((2, array.shape[1], TILE), lambda c, m: (m[0] if row else 0, 0, index)))

    edge_out = out_fixed((rows, width + BLOCK, TILE), BF)
    tail, head = call(
        pack_edges, meta, (1,),
        [
            edge_tile(tokens_t, True, last), edge_tile(cotangent_t, True, last),
            edge_tile(tokens_t, True, 0), edge_tile(cotangent_t, True, 0),
            edge_tile(codes, False, last), edge_tile(codes, False, 0),
        ],
        [edge_out, edge_out], name="pack_edges", us=4,
    )

    small = jnp.stack([bias_inner[0], gain_middle[0], bias_middle[0], bias_conv[0], gain_last[0], bias_last[0]])
    high = lax.reduce_precision(small, 8, 7)
    small = pad_to(jnp.concatenate([high, small - high], axis=0), 0, BLOCK)
    inner_all = pad_to(weight_inner[0].reshape(n_seq, width // n_seq, loc), 1, PIECE)
    inner_all = jnp.concatenate([inner_all, jnp.broadcast_to(small[None], (n_seq,) + small.shape)], axis=1)
    outer_all = pad_to(jnp.transpose(weight_outer[0]).reshape(n_seq, width // n_seq, loc), 1, PIECE)
    conv_all = pad_to(
        jnp.where(
            encoder_side,
            weight_conv_encoder[:4],
            jnp.concatenate([weight_conv_encoder[4:], weight_conv_decoder], axis=0),
        ), 1, 2 * PIECE,
    )

    def gathered(pieces):
        pieces = pad_to(pieces.astype(BF), 2, lanes)
        sent = lax.dynamic_index_in_dim(pieces, seq, 0, keepdims=False)
        if lanes != TILE or n_seq != 4:
            return gather(gather_lanes(sent, "tensor"), "seq")
        near = jnp.stack([flip(sent, "tensor", by) for by in range(1, 4)])
        return [pieces, near] + [flip(near, "seq", by) for by in range(1, 4)]

    def placed_parts(parts):
        if not isinstance(parts, list):
            return parts
        rows_in = parts[0].shape[1]
        return call(
            place_weights, jnp.stack([seq, tensor]).astype(jnp.int32), (1,), [fixed(x) for x in parts],
            [out_fixed((4, rows_in, LANES), BF)], name="place_weights", us=4,
        )[0]

    parts2 = gathered(jnp.concatenate([conv_all, outer_all], axis=1))
    bundle1 = placed_parts(gathered(inner_all))
    before = lax.ppermute(tail, "seq", [(i, i + 1) for i in range(n_seq - 1)])
    after = lax.ppermute(head, "seq", [(i + 1, i) for i in range(n_seq - 1)])
    large = jnp.stack([gain_first[0], bias_first[0], bias_outer[0]], axis=0)
    bundle1b, large2 = flip(bundle1, "pipe", 1), flip(large, "pipe", 1)
    def columns_of(mine, other):
        first, second = jnp.where(encoder_side, mine, other), jnp.where(encoder_side, other, mine)
        return pad_to(jnp.transpose(jnp.concatenate([first, second], axis=0)), 1, TILE)

    def small_of(bundle):
        values = bundle[0, PIECE : PIECE + 12].astype(F32)
        values = (values[:6] + values[6:]).reshape(6, n_tensor, lanes)
        return values[:, :, :loc].reshape(6, inner)

    ph, pd = columns_of(small_of(bundle1), small_of(bundle1b)), columns_of(large, large2)
    first_lane = jnp.arange(inner)
    first_lane = first_lane // loc * lanes + first_lane % loc
    eye = (first_lane[:, None] == jnp.arange(LANES)[None, :]).astype(BF)
    own = (jnp.arange(TILE)[:, None] + tensor * loc == jnp.arange(inner)[None, :]) & (jnp.arange(TILE)[:, None] < loc)
    own = own.astype(BF)
    w_inner = [part(bundle1, PIECE + BLOCK, 0), part(bundle1b, PIECE + BLOCK, 0)]
    none = jnp.zeros((rows, 1, TILE), F32)
    codes = jnp.concatenate(
        [none, before[:, width : width + 1].astype(F32), codes, after[:, width : width + 1].astype(F32), none], axis=2
    ) - 1.0
    code_cols = jnp.broadcast_to(codes[:, 0, :, None], (rows, codes.shape[2], TILE)).astype(BF)
    halo = [fixed(before), fixed(after)]

    ext = length + 4 * TILE
    scr = pltpu.VMEM
    chunk_f = scr((2, width, CHUNK), F32)
    chunk_b = scr((2, width, CHUNK), BF)
    both_b = scr((width, 2 * CHUNK), BF)
    hid_f = scr((2, inner, CHUNK), F32)
    hid_b = scr((2, inner, CHUNK), BF)

    def pds(n):
        return scr((n, width, TILE), F32)

    def phs(n):
        return scr((n, inner, TILE), F32)

    last_ins = [fixed(eye), fixed(own), fixed(pd), fixed(ph)]
    sec_e, xh2_e, dg2_e, inv2_e = call(
        encoder_in, meta, (5,),
        [rows_chunk(tokens_t)] + halo + w_inner + [fixed(eye), fixed(pd), fixed(ph)],
        [out_fixed((rows, ext, LANES), BF), out_chunks(inner, BF), out_chunks(inner, BF), out_chunks(8, F32)],
        [scr((inner, width), BF), pds(2), phs(3), chunk_f, chunk_b, hid_f, hid_b],
        name="encoder_in", us=16,
    )
    parts2, sec_e = lax.optimization_barrier((parts2, sec_e))
    bundle2 = placed_parts(parts2)
    bundle2b = flip(bundle2, "pipe", 1)
    w_conv = [part(bundle2, 2 * PIECE, 0), part(bundle2b, 2 * PIECE, 0)]
    w_outer = [part(bundle2, PIECE, 2), part(bundle2b, PIECE, 2)]
    out_e, xh3_e, dg3_e, inv3_e, third_e, sec_d, xh2_d, dg2_d, inv2_d = call(
        encoder_out, meta, (5,),
        [fixed(sec_e), fixed(codes), fixed(code_cols), rows_chunk(tokens_t)] + halo + w_conv + w_outer + w_inner + last_ins,
        [
            out_chunks(width, F32), out_chunks(inner, BF), out_chunks(inner, BF), out_chunks(8, F32), out_chunks(TILE, BF),
            out_fixed((rows, inner, ext), BF), out_chunks(inner, BF), out_chunks(inner, BF), out_chunks(8, F32),
        ],
        [
            scr((inner, 5 * LANES), BF), scr((width, inner), BF), scr((inner, width), BF), pds(3), phs(6),
            scr((2 * CHUNK, 5 * LANES), BF), hid_f, hid_b, chunk_b, hid_b,
        ],
        name="encoder_out", us=32,
    )
    final = (jax.ShapeDtypeStruct((rows_all, width, length), F32), pl.BlockSpec((2, width, CHUNK), own_index))
    sent = (
        jax.ShapeDtypeStruct((rows, width, length), BF),
        pl.BlockSpec((2, width, CHUNK), lambda c, m: (0, 0, jnp.maximum(c - 1, 0))),
    )
    mine_out, other_out, mixed_d, go_d, gc_d = call(
        decoder_out, meta, (5,),
        [fixed(sec_d), fixed(codes), per_step(out_e), rows_chunk(cotangent_t)] + halo + w_conv + w_outer + last_ins,
        [
            final, sent, out_fixed((rows, inner, ext), BF), out_fixed((width, TILE)), out_fixed((3 * inner, TILE)),
        ],
        [
            scr((inner, 3 * inner), BF), scr((width, inner), BF), scr((inner, width), BF), pds(1), phs(3),
            scr((3 * inner, 2 * CHUNK), BF), hid_f, hid_b, chunk_f, both_b, hid_b, hid_b, hid_b, scr((2, 8, CHUNK), F32),
            pds(1), phs(3),
        ],
        name="decoder_out", us=30,
    )
    grad_d, mixed_e, gi_d, go_e = call(
        decoder_back, meta, (5,),
        [
            fixed(mixed_d), fixed(codes), per_step(xh2_d), per_step(dg2_d), per_step(inv2_d), per_step(out_e),
            rows_chunk(cotangent_t),
        ]
        + halo + [per_step(xh3_e), per_step(dg3_e), per_step(inv3_e), per_step(third_e)]
        + w_conv + w_inner + w_outer + last_ins,
        [out_chunks(width, F32), out_fixed((rows, ext, LANES), BF), out_fixed((width, TILE)), out_fixed((width, TILE))],
        [
            scr((inner, 3 * inner), BF), scr((width, inner), BF), scr((inner, width), BF), pds(2), phs(2),
            scr((3 * inner, 2 * CHUNK), BF), hid_f, hid_b, hid_b, both_b, both_b, chunk_f, pds(3), phs(6),
        ],
        name="decoder_back", us=40,
    )
    mine_grad, other_grad, gi_e, gc_e = call(
        encoder_back, meta, (4,),
        [
            fixed(mixed_e), fixed(sec_e), fixed(code_cols), per_step(xh2_e, 4), per_step(dg2_e, 4), per_step(inv2_e, 4),
            (tokens_t, pl.BlockSpec((2, width, CHUNK), lambda c, m: (m[0], 0, c))), per_step(grad_d, 4),
        ]
        + w_conv + w_inner + last_ins,
        [
            (final[0], pl.BlockSpec((2, width, CHUNK), lambda c, m: (m[0], 0, c))),
            (sent[0], pl.BlockSpec((2, width, CHUNK), lambda c, m: (0, 0, c))),
            out_fixed((width, TILE)), out_fixed((5 * inner, TILE)),
        ],
        [
            scr((inner, 5 * LANES), BF), scr((width, inner), BF), pds(2), phs(1),
            scr((2 * CHUNK, 5 * LANES), BF), scr((2 * CHUNK, 5 * LANES), BF), scr((TILE, 5 * LANES), F32), hid_f, hid_b, both_b, chunk_f, pds(2), phs(3),
        ],
        name="encoder_back", us=32,
    )

    def finish(mine, other):
        block = (1, width // 2, length)
        return jnp.transpose(
            call(
                fill_rows, meta, (2 * rows,),
                [
                    (flip(other, "pipe", 1), pl.BlockSpec(block, lambda c, m: (c // 2, c % 2, 0))),
                    (mine, pl.BlockSpec(memory_space=pl.ANY)),
                ],
                [(final[0], pl.BlockSpec(block, lambda c, m: (rows - rows * m[0] + c // 2, c % 2, 0)))],
                aliases={2: 0}, name="fill_rows", us=7,
            )[0],
            (0, 2, 1),
        )

    section_output = finish(mine_out, other_out)[None]

    taps_rows = 4 * inner
    kept, sent = call(
        pack_grads, meta, (1,), [fixed(x) for x in (gi_e, go_e, gc_e, gi_d, go_d, gc_d)],
        [out_fixed((2 * width + taps_rows, TILE)), out_fixed((2 * width + taps_rows, TILE), BF)],
        name="pack_grads", us=4,
    )
    kept = kept + flip(sent, "pipe", 1).astype(F32)
    parts, section_output = spread_over(kept, "seq", section_output)
    input_gradient = finish(mine_grad, other_grad)[None]
    summed, input_gradient = collect_over(parts, "seq", input_gradient)
    grads_inner, grads_outer = summed[:width], summed[width : 2 * width]
    conv_sum = summed[2 * width :]
    conv_other = flip(conv_sum, "pipe", 1)
    summed_f = [x.astype(F32) for x in (grads_inner, grads_outer)]
    conv_first = jnp.where(encoder_side, conv_sum, conv_other)
    conv_second = jnp.where(encoder_side, conv_other, conv_sum)
    grad_conv_e = jnp.concatenate([conv_first, conv_second[:inner]], axis=0)[:, :loc].astype(F32).reshape(5, inner, loc)
    grad_conv_d = conv_second[inner:, :loc].astype(F32).reshape(3, inner, loc)
    grad_inner = summed_f[0][:, :loc]
    grad_outer = jnp.transpose(summed_f[1][:, :loc])
    wide = [summed_f[0][:, FREE], summed_f[0][:, FREE + 1], summed_f[1][:, FREE]]
    narrow = jnp.concatenate([summed_f[0][:inner, FREE + 2 : FREE + 5], summed_f[1][:inner, FREE + 1 : FREE + 4]], axis=1)
    narrow = jnp.transpose(lax.dynamic_slice_in_dim(narrow, tensor * loc, loc, 0))

    return (
        section_output,
        input_gradient,
        wide[0][None],
        wide[1][None],
        grad_inner[None],
        narrow[2][None],
        narrow[0][None],
        narrow[1][None],
        grad_conv_e,
        grad_conv_d,
        narrow[5][None],
        narrow[3][None],
        narrow[4][None],
        grad_outer[None],
        wide[2][None],
    )


def solution(mesh):
    return jax.shard_map(
        on_device,
        mesh=mesh,
        in_specs=(
            P(None, "seq", None),
            P(None, "seq"),
            P(None, "seq"),
            P(None, "seq", None),
            P("pipe", None),
            P("pipe", None),
            P("pipe", None, "tensor"),
            P("pipe", "tensor"),
            P("pipe", "tensor"),
            P("pipe", "tensor"),
            P(None, None, "tensor"),
            P(None, None, "tensor"),
            P("pipe", "tensor"),
            P("pipe", "tensor"),
            P("pipe", "tensor"),
            P("pipe", "tensor", None),
            P("pipe", None),
        ),
        out_specs=(
            P("pipe", None, "seq", None),
            P("pipe", None, "seq", None),
            P("pipe", None),
            P("pipe", None),
            P("pipe", None, "tensor"),
            P("pipe", "tensor"),
            P("pipe", "tensor"),
            P("pipe", "tensor"),
            P(None, None, "tensor"),
            P(None, None, "tensor"),
            P("pipe", "tensor"),
            P("pipe", "tensor"),
            P("pipe", "tensor"),
            P("pipe", "tensor", None),
            P("pipe", None),
        ),
        check_vma=False,
    )
```

time: 522 us -> 277 us (0.53)
  local copies, waits for them, and re-layouts: 194 us -> 17.2 us
  starting transfers between devices: 84.5 us -> 39.6 us
  other arithmetic: 42.8 us -> 14 us
  Pallas kernels: 152 us -> 178 us
  waiting for transfers between devices: 38 us -> 22.5 us
    dynamic_update_slice x34 -> x3, local copies, waits for them, and re-layouts: 52.8 us -> 0.09 us  [collect_over(): lax.dynamic_update_index_in_dim(result, arrived[by - 1], me ^ by, 0)]
    unnamed x64 -> x42, local copies, waits for them, and re-layouts: 56.5 us -> 3.99 us
    ppermute x46 -> x25, starting transfers between devices: 67 us -> 36.1 us  [flip(): return lax.ppermute(x, axis, [(i, i ^ by) for i in range(count)])]
    ppermute x46 -> x25, waiting for transfers between devices: 38 us -> 11.4 us  [flip(): return lax.ppermute(x, axis, [(i, i ^ by) for i in range(count)])]
    pallas_call x7 -> x11, Pallas kernels: 152 us -> 178 us  [call(): pl.pallas_call(body, grid_spec=pltpu.PrefetchScalarGridSpec(num_scalar_pr...]
    another operation x13 -> x4, local copies, waits for them, and re-layouts: 24.1 us -> 2.45 us  [on_device(): masks = jnp.stack(columns, axis=-1)]
    ppermute x6 -> x2, starting transfers between devices: 17.5 us -> 3.46 us  [the longest x1 1.81 us: on_device(): after = lax.ppermute(head, 'seq', [(i + 1, i) for i in range(n_seq - 1)])]
    dynamic_slice x4 -> x0, local copies, waits for them, and re-layouts: 13.3 us -> none  [the longest x1 12.3 us: mine_rows(): return lax.dynamic_slice_in_dim(array, pipe * rows, rows, 0)]
  transfers between devices with their start and end apart: 52 -> 27, of which waited for: 12 -> 8; matrix products, arithmetic and copies ran while one was open for 40% -> 8% of each run, Pallas kernels for 4% -> 41%
where the time goes in v2:
time: 277 us; the launch traced here: 273 us
  Pallas kernels  178 us (64%)
  starting transfers between devices  39.6 us (14%)
  waiting for transfers between devices  22.5 us (8%)
  local copies, waits for them, and re-layouts  17.2 us (6%)
  other arithmetic  14 us (5%)
    pallas_call x11, Pallas kernels, call(): pl.pallas_call(body, grid_spec=pltpu.PrefetchScalarGridSpec(num_scalar_pr...  178 us
    ppermute x25, starting transfers between devices, flip(): return lax.ppermute(x, axis, [(i, i ^ by) for i in range(count)])  36.1 us
    ppermute x25, waiting for transfers between devices, flip(): return lax.ppermute(x, axis, [(i, i ^ by) for i in range(count)])  11.4 us
    ppermute x1, waiting for transfers between devices, on_device(): after = lax.ppermute(head, 'seq', [(i + 1, i) for i in range(n_seq - 1)])  11.1 us
  transfers between devices with their start and end apart: 27, of which 8 were waited for; matrix products, arithmetic and copies ran while one was open for 8% of the time, Pallas kernels for 41%

profile of v2, /device:TPU:1, one launch (start us, length us, event | category | flops | bytes accessed | tf_op | source)
XLA Modules:
  0.0 272.8 jit_solution(11965601258052136677)
XLA Ops:
  3.6 2.2 collective-permute-start.8
  5.8 2.3 collective-permute-start.9
  11.9 3.2 %collective-permute-start.1 = (bf16[624,128]{1,0:T(8,128)(2,1)S(1)}, bf16[624,128]{1,0:T(8,128)(2,1)S(1)}, u32[]{:S(2)}, u32[]{:S(2)}) collective-permute-start(bf16[624,128]{1,0:T(8,128)(2,1)S(1)} %dynamic-slice_bitcast_fusion.3), channel_id=1, source_target_pairs={{0,2},{1,3},{2,0},{3,1},{4,6},{5,7},{6,4},{7,5},{8,10},{9,11},{10,... | collective-permute-start | bytes 479240 | tf_op jit(solution)/shard_map/ppermute | solution.py:626
  18.0 3.7 %pack_edges.1 = (bf16[2,816,128]{2,1,0:T(8,128)(2,1)}, bf16[2,816,128]{2,1,0:T(8,128)(2,1)}) custom-call(s32[2]{0:T(128)} %pad_add_fusion.meta, f32[4,800,1024]{2,1,0:T(8,128)} %bitcast.86, f32[4,800,1024]{2,1,0:T(8,128)} %bitcast.82, f32[4,800,1024]{2,1,0:T(8,128)} %bitcast.87, f32[4,800,1024]{2,1,0:T(8,128)} %bitcast.83, ...), custom_call_target="tpu_custom_call" | custom-call | flops 4000000000 | bytes 14000000 | tf_op jit(solution)/shard_map/pack_edges/pallas_call | solution.py:574
  28.2 6.5 %collective-permute-start.15 = (f32[3,800]{1,0:T(4,128)S(1)}, f32[3,800]{1,0:T(4,128)S(1)}, u32[]{:S(2)}, u32[]{:S(2)}) collective-permute-start(f32[3,800]{1,0:T(4,128)S(1)} %pad_maximum_fusion.5), channel_id=1, source_target_pairs={{0,16},{16,0},{1,17},{17,1},{2,18},{18,2},{3,19},{19,3},{4,20},{20... | collective-permute-start | bytes 28808 | tf_op jit(solution)/shard_map/ppermute | solution.py:626
  35.4 3.0 %place_weights.2.a_ref.ai_ref = bf16[4,224,512]{2,1,0:T(8,128)(2,1)} custom-call(s32[2]{0:T(128)} %pad_add_fusion.1.place, bf16[4,224,128]{2,1,0:T(8,128)(2,1)} %pad.39.own_ref, bf16[3,224,128]{2,1,0:T(8,128)(2,1)} %copy-done.3, bf16[3,224,128]{2,1,0:T(8,128)(2,1)} %copy-done.14, bf16[3,224,128]{2,1,0:T(8,128)(2,1)} %copy-done.15, ...), custom_call_target="tpu_custom_call" | custom-call | flops 4000000000 | bytes 14000000 | tf_op jit(solution)/shard_map/place_weights/pallas_call | solution.py:574
  40.0 1.7 collective-permute-start.6
  42.7 1.8 collective-permute-start.7
  44.6 2.9 %collective-permute-start.3 = (bf16[3,624,128]{2,1,0:T(8,128)(2,1)S(1)}, bf16[3,624,128]{2,1,0:T(8,128)(2,1)}, u32[]{:S(2)}, u32[]{:S(2)}) collective-permute-start(bf16[3,624,128]{2,1,0:T(8,128)(2,1)S(1)} %pad_maximum_fusion.1.refs_0_), channel_id=1, source_target_pairs={{0,4},{4,0},{8,12},{12,8},{1,5},{5,1},{9,13},{13,9},{2,6},{6,2},{1... | collective-permute-start | bytes 1437704 | tf_op jit(solution)/shard_map/ppermute | solution.py:626
  51.7 11.1 %collective-permute-done.7.after_ref = bf16[2,816,128]{2,1,0:T(8,128)(2,1)S(1)} collective-permute-done((bf16[2,816,128]{2,1,0:T(8,128)(2,1)S(1)}, bf16[2,816,128]{2,1,0:T(8,128)(2,1)S(1)}, u32[]{:S(2)}, u32[]{:S(2)}) %collective-permute-start.7) | collective-permute-done | bytes 417824 | tf_op jit(solution)/shard_map/ppermute | solution.py:752
  63.6 15.9 %encoder_in.1 = (bf16[2,1536,512]{2,1,0:T(8,128)(2,1)}, bf16[10,400,256]{2,1,0:T(8,128)(2,1)}, bf16[10,400,256]{2,1,0:T(8,128)(2,1)}, f32[10,8,256]{2,1,0:T(8,128)}) custom-call(s32[2]{0:T(128)} %pad_add_fusion.meta, f32[4,800,1024]{2,1,0:T(8,128)} %bitcast.88, bf16[2,816,128]{2,1,0:T(8,128)(2,1)} %copy-done.10, bf16[2,816,128]{2,1,0:T(8,128)(2,1)} %copy-done.11, ...), custom_call_target="tpu_custom_call" | custom-call | flops 16000000000 | bytes 56000000 | tf_op jit(solution)/shard_map/encoder_in/pallas_call | solution.py:574
  79.6 4.3 %place_weights.3.a_ref.ao_ref = bf16[4,624,512]{2,1,0:T(8,128)(2,1)} custom-call(s32[2]{0:T(128)} %pad_add_fusion.1.place, bf16[4,624,128]{2,1,0:T(8,128)(2,1)} %pad.36.own_ref, bf16[3,624,128]{2,1,0:T(8,128)(2,1)} %copy-done.1, bf16[3,624,128]{2,1,0:T(8,128)(2,1)} %collective-permute-done.3.refs_1_, bf16[3,624,128]{2,1,0:T(8,128)(2,1)} %collective-permute-done.4.refs_2_, ...), custom_call_target="tpu_custom_call" | custom-call | flops 4000000000 | bytes 14000000 | tf_op jit(solution)/shard_map/place_weights/pallas_call | solution.py:574
  89.7 1.7 broadcast_in_dim.61.col_ref
  91.5 32.7 %encoder_out.1 = (f32[10,800,256]{2,1,0:T(8,128)}, bf16[10,400,256]{2,1,0:T(8,128)(2,1)}, bf16[10,400,256]{2,1,0:T(8,128)(2,1)}, f32[10,8,256]{2,1,0:T(8,128)}, ...) custom-call(s32[2]{0:T(128)} %pad_add_fusion.meta, ...), custom_call_target="tpu_custom_call" | custom-call | flops 32000000000 | bytes 112000000 | tf_op jit(solution)/shard_map/encoder_out/pallas_call | solution.py:574
  124.2 29.8 %decoder_out.1 = (f32[4,800,1024]{2,1,0:T(8,128)}, bf16[2,800,1024]{2,1,0:T(8,128)(2,1)}, bf16[2,400,1536]{2,1,0:T(8,128)(2,1)}, f32[800,128]{1,0:T(8,128)}, f32[1200,128]{1,0:T(8,128)}) custom-call(s32[2]{0:T(128)} %pad_add_fusion.meta, bf16[2,400,1536]{2,1,0:T(8,128)(2,1)} %get-tuple-element.68.sec_ref, f32[2,1,1536]{2,1,0:T(1,128)} %broadcast_add_fusion.code_ref, ...), custom_call_target="tpu_custom_call" | custom-call | flops 30000001024 | bytes 105000000 | tf_op jit(solution)/shard_map/decoder_out/pallas_call | solution.py:574
  154.4 41.0 %decoder_back.1 = (f32[10,800,256]{2,1,0:T(8,128)}, bf16[2,1536,512]{2,1,0:T(8,128)(2,1)}, f32[800,128]{1,0:T(8,128)}, f32[800,128]{1,0:T(8,128)}) custom-call(s32[2]{0:T(128)} %pad_add_fusion.meta, bf16[2,400,1536]{2,1,0:T(8,128)(2,1)} %get-tuple-element.70.mixed_ref, f32[2,1,1536]{2,1,0:T(1,128)} %broadcast_add_fusion.code_ref, ...), custom_call_target="tpu_custom_call" | custom-call | flops 40000000000 | bytes 140000000 | tf_op jit(solution)/shard_map/decoder_back/pallas_call | solution.py:574
  195.4 31.8 %encoder_back.1 = (f32[4,800,1024]{2,1,0:T(8,128)}, bf16[2,800,1024]{2,1,0:T(8,128)(2,1)}, f32[800,128]{1,0:T(8,128)}, f32[2000,128]{1,0:T(8,128)}) custom-call(s32[2]{0:T(128)} %pad_add_fusion.meta, bf16[2,1536,512]{2,1,0:T(8,128)(2,1)} %get-tuple-element.78.mixed_ref, bf16[2,1536,512]{2,1,0:T(8,128)(2,1)} %get-tuple-element.62.sec_ref, ...), custom_call_target="tpu_custom_call" | custom-call | flops 32000000000 | bytes 112000000 | tf_op jit(solution)/shard_map/encoder_back/pallas_call | solution.py:574
  227.4 4.2 %pack_grads.1 = (f32[3200,128]{1,0:T(8,128)}, bf16[3200,128]{1,0:T(8,128)(2,1)}) custom-call(s32[2]{0:T(128)} %pad_add_fusion.meta, f32[800,128]{1,0:T(8,128)} %get-tuple-element.83.gie, f32[800,128]{1,0:T(8,128)} %get-tuple-element.84.goe, f32[2000,128]{1,0:T(8,128)} %get-tuple-element.85.gce, f32[800,128]{1,0:T(8,128)} %get-tuple-element.86.gid, ...), custom_call_target="tpu_custom_call" | custom-call | flops 4000000000 | bytes 14000000 | tf_op jit(solution)/shard_map/pack_grads/pallas_call | solution.py:574
  232.0 2.5 collective-permute-done.17
  236.2 3.8 %collective-permute-start.18 = (bf16[800,128]{1,0:T(8,128)(2,1)S(1)}, bf16[800,128]{1,0:T(8,128)(2,1)S(1)}, u32[]{:S(2)}, u32[]{:S(2)}) collective-permute-start(bf16[800,128]{1,0:T(8,128)(2,1)S(1)} %get-tuple-element.158), channel_id=1, source_target_pairs={{0,4},{4,0},{8,12},{12,8},{1,5},{5,1},{9,13},{13,9},{2,6},{6,2},{1... | collective-permute-start | bytes 614408 | tf_op jit(solution)/shard_map/ppermute | solution.py:626
  242.1 5.8 %fill_rows.2 = f32[4,800,1024]{2,1,0:T(8,128)} custom-call(s32[2]{0:T(128)} %pad_add_fusion.meta, bf16[2,800,1024]{2,1,0:T(8,128)(2,1)} %collective-permute-done.21.recv_ref, f32[4,800,1024]{2,1,0:T(8,128)} %get-tuple-element.92.final_ref), custom_call_target="tpu_custom_call", output_to_operand_aliasing={{}: (2, {})} | custom-call | flops 7000000000 | bytes 24500000 | tf_op jit(solution)/shard_map/fill_rows/pallas_call | solution.py:574
  249.6 2.0 collective-permute-done.20
  254.6 5.8 %fill_rows.3 = f32[4,800,1024]{2,1,0:T(8,128)} custom-call(s32[2]{0:T(128)} %pad_add_fusion.meta, bf16[2,800,1024]{2,1,0:T(8,128)(2,1)} %collective-permute-done.25.recv_ref, f32[4,800,1024]{2,1,0:T(8,128)} %get-tuple-element.98.final_ref), custom_call_target="tpu_custom_call", output_to_operand_aliasing={{}: (2, {})} | custom-call | flops 7000000000 | bytes 24500000 | tf_op jit(solution)/shard_map/fill_rows/pallas_call | solution.py:574
  262.3 2.1 collective-permute-start.26
  (163 shorter events, 49.6 us)
Async XLA Ops:
  3.6 18.8 %collective-permute-start.8 = (bf16[224,128]{1,0:T(8,128)(2,1)S(1)}, bf16[224,128]{1,0:T(8,128)(2,1)S(1)}, u32[]{:S(2)}, u32[]{:S(2)}) collective-permute-start(bf16[224,128]{1,0:T(8,128)(2,1)S(1)} %dynamic-slice_bitcast_fusion.4), channel_id=1, source_target_pairs={{0,1},{1,0},{2,3},{3,2},{4,5},{5,4},{6,7},{7,6},{8,9},{9,8},{10,11... | collective-permute-start | bytes 172040 | tf_op jit(solution)/shard_map/ppermute | solution.py:626
  5.8 16.6 %collective-permute-start.9 = (bf16[224,128]{1,0:T(8,128)(2,1)S(1)}, bf16[224,128]{1,0:T(8,128)(2,1)S(1)}, u32[]{:S(2)}, u32[]{:S(2)}) collective-permute-start(bf16[224,128]{1,0:T(8,128)(2,1)S(1)} %dynamic-slice_bitcast_fusion.4), channel_id=1, source_target_pairs={{0,2},{1,3},{2,0},{3,1},{4,6},{5,7},{6,4},{7,5},{8,10},{9,11},{10,... | collective-permute-start | bytes 172040 | tf_op jit(solution)/shard_map/ppermute | solution.py:626
  8.1 14.3 %collective-permute-start.10 = (bf16[224,128]{1,0:T(8,128)(2,1)S(1)}, bf16[224,128]{1,0:T(8,128)(2,1)S(1)}, u32[]{:S(2)}, u32[]{:S(2)}) collective-permute-start(bf16[224,128]{1,0:T(8,128)(2,1)S(1)} %dynamic-slice_bitcast_fusion.4), channel_id=1, source_target_pairs={{0,3},{1,2},{2,1},{3,0},{4,7},{5,6},{6,5},{7,4},{8,11},{9,10},{10,... | collective-permute-start | bytes 172040 | tf_op jit(solution)/shard_map/ppermute | solution.py:626
  11.5 31.2 %collective-permute-start = (bf16[624,128]{1,0:T(8,128)(2,1)S(1)}, bf16[624,128]{1,0:T(8,128)(2,1)S(1)}, u32[]{:S(2)}, u32[]{:S(2)}) collective-permute-start(bf16[624,128]{1,0:T(8,128)(2,1)S(1)} %dynamic-slice_bitcast_fusion.3), channel_id=1, source_target_pairs={{0,1},{1,0},{2,3},{3,2},{4,5},{5,4},{6,7},{7,6},{8,9},{9,8},{10,11... | collective-permute-start | bytes 479240 | tf_op jit(solution)/shard_map/ppermute | solution.py:626
  11.9 32.6 %collective-permute-start.1 = (bf16[624,128]{1,0:T(8,128)(2,1)S(1)}, bf16[624,128]{1,0:T(8,128)(2,1)S(1)}, u32[]{:S(2)}, u32[]{:S(2)}) collective-permute-start(bf16[624,128]{1,0:T(8,128)(2,1)S(1)} %dynamic-slice_bitcast_fusion.3), channel_id=1, source_target_pairs={{0,2},{1,3},{2,0},{3,1},{4,6},{5,7},{6,4},{7,5},{8,10},{9,11},{10,... | collective-permute-start | bytes 479240 | tf_op jit(solution)/shard_map/ppermute | solution.py:626
  24.9 9.8 %collective-permute-start.13 = (bf16[3,224,128]{2,1,0:T(8,128)(2,1)S(1)}, bf16[3,224,128]{2,1,0:T(8,128)(2,1)S(1)}, u32[]{:S(2)}, u32[]{:S(2)}) collective-permute-start(bf16[3,224,128]{2,1,0:T(8,128)(2,1)S(1)} %pad_maximum_fusion.2.refs_0_), channel_id=1, source_target_pairs={{0,12},{4,8},{8,4},{12,0},{1,13},{5,9},{9,5},{13,1},{2,14},{6,10},... | collective-permute-start | bytes 516104 | tf_op jit(solution)/shard_map/ppermute | solution.py:626
  26.7 17.8 %collective-permute-start.2 = (bf16[624,128]{1,0:T(8,128)(2,1)S(1)}, bf16[624,128]{1,0:T(8,128)(2,1)S(1)}, u32[]{:S(2)}, u32[]{:S(2)}) collective-permute-start(bf16[624,128]{1,0:T(8,128)(2,1)S(1)} %dynamic-slice_bitcast_fusion.3), channel_id=1, source_target_pairs={{0,3},{1,2},{2,1},{3,0},{4,7},{5,6},{6,5},{7,4},{8,11},{9,10},{10,... | collective-permute-start | bytes 479240 | tf_op jit(solution)/shard_map/ppermute | solution.py:626
  28.2 11.8 %collective-permute-start.15 = (f32[3,800]{1,0:T(4,128)S(1)}, f32[3,800]{1,0:T(4,128)S(1)}, u32[]{:S(2)}, u32[]{:S(2)}) collective-permute-start(f32[3,800]{1,0:T(4,128)S(1)} %pad_maximum_fusion.5), channel_id=1, source_target_pairs={{0,16},{16,0},{1,17},{17,1},{2,18},{18,2},{3,19},{19,3},{4,20},{20... | collective-permute-start | bytes 28808 | tf_op jit(solution)/shard_map/ppermute | solution.py:626
  38.4 11.1 %collective-permute-start.14 = (bf16[4,224,512]{2,1,0:T(8,128)(2,1)}, bf16[4,224,512]{2,1,0:T(8,128)(2,1)S(1)}, u32[]{:S(2)}, u32[]{:S(2)}) collective-permute-start(bf16[4,224,512]{2,1,0:T(8,128)(2,1)} %place_weights.2.a_ref.ai_ref), channel_id=1, source_target_pairs={{0,16},{16,0},{1,17},{17,1},{2,18},{18,2},{3,19},{19,3},{4,20},{20... | collective-permute-start | bytes 2752520 | tf_op jit(solution)/shard_map/ppermute | solution.py:626
  40.0 11.7 %collective-permute-start.6 = (bf16[2,816,128]{2,1,0:T(8,128)(2,1)}, bf16[2,816,128]{2,1,0:T(8,128)(2,1)S(1)}, u32[]{:S(2)}, u32[]{:S(2)}) collective-permute-start(bf16[2,816,128]{2,1,0:T(8,128)(2,1)} %get-tuple-element.59), channel_id=1, source_target_pairs={{0,4},{4,8},{8,12},{1,5},{5,9},{9,13},{2,6},{6,10},{10,14},{3,7},{... | collective-permute-start | bytes 1253384 | tf_op jit(solution)/shard_map/ppermute | solution.py:751
  42.7 20.1 %collective-permute-start.7 = (bf16[2,816,128]{2,1,0:T(8,128)(2,1)S(1)}, bf16[2,816,128]{2,1,0:T(8,128)(2,1)S(1)}, u32[]{:S(2)}, u32[]{:S(2)}) collective-permute-start(bf16[2,816,128]{2,1,0:T(8,128)(2,1)S(1)} %copy-done.13), channel_id=1, source_target_pairs={{4,0},{8,4},{12,8},{5,1},{9,5},{13,9},{6,2},{10,6},{14,10},{7,3},{... | collective-permute-start | bytes 1253384 | tf_op jit(solution)/shard_map/ppermute | solution.py:752
  44.6 35.0 %collective-permute-start.3 = (bf16[3,624,128]{2,1,0:T(8,128)(2,1)S(1)}, bf16[3,624,128]{2,1,0:T(8,128)(2,1)}, u32[]{:S(2)}, u32[]{:S(2)}) collective-permute-start(bf16[3,624,128]{2,1,0:T(8,128)(2,1)S(1)} %pad_maximum_fusion.1.refs_0_), channel_id=1, source_target_pairs={{0,4},{4,0},{8,12},{12,8},{1,5},{5,1},{9,13},{13,9},{2,6},{6,2},{1... | collective-permute-start | bytes 1437704 | tf_op jit(solution)/shard_map/ppermute | solution.py:626
  47.5 32.1 %collective-permute-start.4 = (bf16[3,624,128]{2,1,0:T(8,128)(2,1)S(1)}, bf16[3,624,128]{2,1,0:T(8,128)(2,1)}, u32[]{:S(2)}, u32[]{:S(2)}) collective-permute-start(bf16[3,624,128]{2,1,0:T(8,128)(2,1)S(1)} %pad_maximum_fusion.1.refs_0_), channel_id=1, source_target_pairs={{0,8},{4,12},{8,0},{12,4},{1,9},{5,13},{9,1},{13,5},{2,10},{6,14},... | collective-permute-start | bytes 1437704 | tf_op jit(solution)/shard_map/ppermute | solution.py:626
  49.5 30.1 %collective-permute-start.5 = (bf16[3,624,128]{2,1,0:T(8,128)(2,1)S(1)}, bf16[3,624,128]{2,1,0:T(8,128)(2,1)}, u32[]{:S(2)}, u32[]{:S(2)}) collective-permute-start(bf16[3,624,128]{2,1,0:T(8,128)(2,1)S(1)} %pad_maximum_fusion.1.refs_0_), channel_id=1, source_target_pairs={{0,12},{4,8},{8,4},{12,0},{1,13},{5,9},{9,5},{13,1},{2,14},{6,10},... | collective-permute-start | bytes 1437704 | tf_op jit(solution)/shard_map/ppermute | solution.py:626
  83.9 5.8 %collective-permute-start.16 = (bf16[4,624,512]{2,1,0:T(8,128)(2,1)}, bf16[4,624,512]{2,1,0:T(8,128)(2,1)S(1)}, u32[]{:S(2)}, u32[]{:S(2)}) collective-permute-start(bf16[4,624,512]{2,1,0:T(8,128)(2,1)} %place_weights.3.a_ref.ao_ref), channel_id=1, source_target_pairs={{0,16},{16,0},{1,17},{17,1},{2,18},{18,2},{3,19},{19,3},{4,20},{20... | collective-permute-start | bytes 7667720 | tf_op jit(solution)/shard_map/ppermute | solution.py:626
  153.9 88.2 %collective-permute-start.21 = (bf16[2,800,1024]{2,1,0:T(8,128)(2,1)}, bf16[2,800,1024]{2,1,0:T(8,128)(2,1)}, u32[]{:S(2)}, u32[]{:S(2)}) collective-permute-start(bf16[2,800,1024]{2,1,0:T(8,128)(2,1)} %get-tuple-element.91), channel_id=1, source_target_pairs={{0,16},{16,0},{1,17},{17,1},{2,18},{18,2},{3,19},{19,3},{4,20},{20... | collective-permute-start | bytes 9830408 | tf_op jit(solution)/shard_map/ppermute | solution.py:626
  227.2 27.4 %collective-permute-start.25 = (bf16[2,800,1024]{2,1,0:T(8,128)(2,1)}, bf16[2,800,1024]{2,1,0:T(8,128)(2,1)}, u32[]{:S(2)}, u32[]{:S(2)}) collective-permute-start(bf16[2,800,1024]{2,1,0:T(8,128)(2,1)} %get-tuple-element.97), channel_id=1, source_target_pairs={{0,16},{16,0},{1,17},{17,1},{2,18},{18,2},{3,19},{19,3},{4,20},{20... | collective-permute-start | bytes 9830408 | tf_op jit(solution)/shard_map/ppermute | solution.py:626
  236.2 11.8 %collective-permute-start.18 = (bf16[800,128]{1,0:T(8,128)(2,1)S(1)}, bf16[800,128]{1,0:T(8,128)(2,1)S(1)}, u32[]{:S(2)}, u32[]{:S(2)}) collective-permute-start(bf16[800,128]{1,0:T(8,128)(2,1)S(1)} %get-tuple-element.158), channel_id=1, source_target_pairs={{0,4},{4,0},{8,12},{12,8},{1,5},{5,1},{9,13},{13,9},{2,6},{6,2},{1... | collective-permute-start | bytes 614408 | tf_op jit(solution)/shard_map/ppermute | solution.py:626
  240.0 9.6 %collective-permute-start.19 = (bf16[800,128]{1,0:T(8,128)(2,1)S(1)}, bf16[800,128]{1,0:T(8,128)(2,1)S(1)}, u32[]{:S(2)}, u32[]{:S(2)}) collective-permute-start(bf16[800,128]{1,0:T(8,128)(2,1)S(1)} %get-tuple-element.157), channel_id=1, source_target_pairs={{0,8},{4,12},{8,0},{12,4},{1,9},{5,13},{9,1},{13,5},{2,10},{6,14},... | collective-permute-start | bytes 614408 | tf_op jit(solution)/shard_map/ppermute | solution.py:626
  241.0 10.6 %collective-permute-start.20 = (bf16[800,128]{1,0:T(8,128)(2,1)S(1)}, bf16[800,128]{1,0:T(8,128)(2,1)S(1)}, u32[]{:S(2)}, u32[]{:S(2)}) collective-permute-start(bf16[800,128]{1,0:T(8,128)(2,1)S(1)} %get-tuple-element.156), channel_id=1, source_target_pairs={{0,12},{4,8},{8,4},{12,0},{1,13},{5,9},{9,5},{13,1},{2,14},{6,10},... | collective-permute-start | bytes 614408 | tf_op jit(solution)/shard_map/ppermute | solution.py:626
  251.8 8.6 %collective-permute-start.22 = (bf16[800,128]{1,0:T(8,128)(2,1)S(1)}, bf16[800,128]{1,0:T(8,128)(2,1)S(1)}, u32[]{:S(2)}, u32[]{:S(2)}) collective-permute-start(bf16[800,128]{1,0:T(8,128)(2,1)S(1)} %get-tuple-element.151), channel_id=1, source_target_pairs={{0,4},{4,0},{8,12},{12,8},{1,5},{5,1},{9,13},{13,9},{2,6},{6,2},{1... | collective-permute-start | bytes 614408 | tf_op jit(solution)/shard_map/ppermute | solution.py:626
  252.2 8.2 %collective-permute-start.23 = (bf16[800,128]{1,0:T(8,128)(2,1)S(1)}, bf16[800,128]{1,0:T(8,128)(2,1)S(1)}, u32[]{:S(2)}, u32[]{:S(2)}) collective-permute-start(bf16[800,128]{1,0:T(8,128)(2,1)S(1)} %get-tuple-element.151), channel_id=1, source_target_pairs={{0,8},{4,12},{8,0},{12,4},{1,9},{5,13},{9,1},{13,5},{2,10},{6,14},... | collective-permute-start | bytes 614408 | tf_op jit(solution)/shard_map/ppermute | solution.py:626
  253.3 8.7 %collective-permute-start.24 = (bf16[800,128]{1,0:T(8,128)(2,1)S(1)}, bf16[800,128]{1,0:T(8,128)(2,1)S(1)}, u32[]{:S(2)}, u32[]{:S(2)}) collective-permute-start(bf16[800,128]{1,0:T(8,128)(2,1)S(1)} %get-tuple-element.151), channel_id=1, source_target_pairs={{0,12},{4,8},{8,4},{12,0},{1,13},{5,9},{9,5},{13,1},{2,14},{6,10},... | collective-permute-start | bytes 614408 | tf_op jit(solution)/shard_map/ppermute | solution.py:626
  262.3 8.2 %collective-permute-start.26 = (bf16[1600,128]{1,0:T(8,128)(2,1)S(1)}, bf16[1600,128]{1,0:T(8,128)(2,1)S(1)}, u32[]{:S(2)}, u32[]{:S(2)}) collective-permute-start(bf16[1600,128]{1,0:T(8,128)(2,1)S(1)} %bitcast.96), channel_id=1, source_target_pairs={{0,16},{16,0},{1,17},{17,1},{2,18},{18,2},{3,19},{19,3},{4,20},{20... | collective-permute-start | bytes 1228808 | tf_op jit(solution)/shard_map/ppermute | solution.py:626
  (20 other events, 162.5 us)
